TPU v7x, 32 devices: a whole 2x2x4 slice. The times are simulated.
32 devices in a mesh: gx: 8 (over y, x, core), sa: 4 (over z).
Axes of the slice: x: 2, y: 2, z: 4, core: 2. Of those that a mesh axis runs over, the one named last changes fastest.
Arguments:
- field_in: bfloat16 [4, 8, 256, 1024], P('sa', 'gx'), may hold values from -6 to 6
- cotangent: bfloat16 [4, 8, 256, 1024], P('sa', 'gx'), may hold values from -6 to 6
- mode_weights: bfloat16 [32, 512, 64, 128], P(None, 'gx'), may hold values from -1 to 1
- point_weights: bfloat16 [64, 64], replicated, may hold values from -0.75 to 0.75
Outputs:
- field_out: bfloat16 [4, 8, 256, 1024], P('sa', 'gx')
- field_grad: bfloat16 [4, 8, 256, 1024], P('sa', 'gx')
- weight_grad: float32 [32, 512, 64, 128], P('sa', 'gx')
All inputs are finite; a program needn't handle non-finite values.
Results may differ from a plain program's by a relative error of at most 0.018.
Values may be sent and summed in bfloat16 or wider, within the bound.
A program may use at most 128 MiB of HBM per device.

v0:
```python
import functools
import math

import jax
import jax.numpy as jnp
import numpy as np
from jax import lax
from jax.experimental import pallas as pl
from jax.experimental.pallas import tpu as pltpu
from jax.sharding import PartitionSpec as P

KY = 32
KZ = 16


HIGHEST_PREC = lax.Precision.HIGHEST
GELU_COEF = 0.044715


def partner(block, axis, distance):
    count = lax.axis_size(axis)
    route = []
    for low in range(count):
        high = low | 1 << distance
        if high != low and high < count:
            route += [(low, high), (high, low)]
    return lax.ppermute(block, axis, route)


def angles(freq_count, grid_count):
    frequency = jnp.arange(freq_count, dtype=jnp.int32) - freq_count // 2
    places = jnp.arange(grid_count, dtype=jnp.int32)
    turn_index = jnp.mod(frequency[:, None] * places[None, :], grid_count)
    return turn_index.astype(jnp.float32) * (2.0 * math.pi / grid_count)


def gelu_parts(pre_act):
    root_const = math.sqrt(2.0 / math.pi)
    inner_arg = root_const * (pre_act + GELU_COEF * pre_act * pre_act * pre_act)
    tangent = jnp.tanh(inner_arg)
    activated = 0.5 * pre_act * (1.0 + tangent)
    gelu_slope = 0.5 * (1.0 + tangent) + 0.5 * pre_act * (1.0 - tangent * tangent) * root_const * (
        1.0 + 3.0 * GELU_COEF * pre_act * pre_act
    )
    return (activated, gelu_slope)


def along_z_forward(data_in, table_z):
    return jnp.einsum("pyzc,kz->pykc", data_in, table_z, precision=HIGHEST_PREC)


def along_z_inverse(data_in, table_z):
    return jnp.einsum("pykc,kz->pyzc", data_in, table_z, precision=HIGHEST_PREC)


def forward_yz(local_field, channels):
    planes, y_count, last_width = local_field.shape
    z_count = last_width // channels
    theta_y = angles(KY, y_count)
    table_y = jnp.concatenate([jnp.cos(theta_y), -jnp.sin(theta_y)], 0).astype(jnp.bfloat16)
    first_pass = jnp.einsum("fy,pyq->pfq", table_y, local_field, preferred_element_type=jnp.float32)
    first_pass = first_pass.reshape(planes, 2, KY, z_count, channels)
    theta_z = angles(KZ, z_count)
    cos_z = jnp.cos(theta_z)
    sin_z = jnp.sin(theta_z)
    real_in = first_pass[:, 0]
    imag_in = first_pass[:, 1]
    real_out = along_z_forward(real_in, cos_z) + along_z_forward(imag_in, sin_z)
    imag_out = along_z_forward(imag_in, cos_z) - along_z_forward(real_in, sin_z)
    mode_data = jnp.concatenate([real_out, imag_out], -1)
    return mode_data.reshape(planes, KY * KZ, 2 * channels).astype(jnp.bfloat16)


def forward_x(mode_data, kx_count, norm_scale):
    x_length, mode_block, pair_width = mode_data.shape
    channels = pair_width // 2
    theta_x = angles(kx_count, x_length)
    flat_data = mode_data.reshape(x_length, mode_block * pair_width)
    cos_part = jnp.dot(
        jnp.cos(theta_x).astype(jnp.bfloat16), flat_data, preferred_element_type=jnp.float32
    ).reshape(kx_count, mode_block, pair_width)
    sin_part = jnp.dot(
        jnp.sin(theta_x).astype(jnp.bfloat16), flat_data, preferred_element_type=jnp.float32
    ).reshape(kx_count, mode_block, pair_width)
    real_out = cos_part[..., :channels] + sin_part[..., channels:]
    imag_out = cos_part[..., channels:] - sin_part[..., :channels]
    return (jnp.concatenate([real_out, imag_out], -1) * norm_scale).astype(jnp.bfloat16)


def inverse_x(mixed_modes, x_length):
    kx_count, mode_block, pair_width = mixed_modes.shape
    channels = pair_width // 2
    theta_x = angles(kx_count, x_length).T
    flat_data = mixed_modes.reshape(kx_count, mode_block * pair_width)
    cos_part = jnp.dot(
        jnp.cos(theta_x).astype(jnp.bfloat16), flat_data, preferred_element_type=jnp.float32
    ).reshape(x_length, mode_block, pair_width)
    sin_part = jnp.dot(
        jnp.sin(theta_x).astype(jnp.bfloat16), flat_data, preferred_element_type=jnp.float32
    ).reshape(x_length, mode_block, pair_width)
    real_out = cos_part[..., :channels] - sin_part[..., channels:]
    imag_out = cos_part[..., channels:] + sin_part[..., :channels]
    return jnp.concatenate([real_out, imag_out], -1).astype(jnp.bfloat16)


def inverse_yz(planes_data, y_count, z_count, norm_scale):
    planes, mode_total, pair_width = planes_data.shape
    channels = pair_width // 2
    wide_data = planes_data.astype(jnp.float32).reshape(planes, KY, KZ, pair_width)
    real_in = wide_data[..., :channels]
    imag_in = wide_data[..., channels:]
    theta_z = angles(KZ, z_count)
    cos_z = jnp.cos(theta_z)
    sin_z = jnp.sin(theta_z)
    real_mid = along_z_inverse(real_in, cos_z) - along_z_inverse(imag_in, sin_z)
    imag_mid = along_z_inverse(imag_in, cos_z) + along_z_inverse(real_in, sin_z)
    stacked = jnp.concatenate([real_mid, imag_mid], 1).reshape(planes, 2 * KY, z_count * channels)
    theta_y = angles(KY, y_count)
    table_y = jnp.concatenate([jnp.cos(theta_y), -jnp.sin(theta_y)], 0)
    return jnp.einsum("pfq,fy->pyq", stacked, table_y, precision=HIGHEST_PREC) * norm_scale


def mix_forward(coeffs, weights_local):
    channels = weights_local.shape[2]
    real_part = jnp.einsum(
        "kmc,kmcp->kmp", coeffs[..., :channels], weights_local, preferred_element_type=jnp.float32
    )
    imag_part = jnp.einsum(
        "kmc,kmcp->kmp", coeffs[..., channels:], weights_local, preferred_element_type=jnp.float32
    )
    out_real = real_part[..., :channels] - imag_part[..., channels:]
    out_imag = real_part[..., channels:] + imag_part[..., :channels]
    return jnp.concatenate([out_real, out_imag], -1).astype(jnp.bfloat16)


def mix_backward(coeffs, weights_local):
    channels = weights_local.shape[2]
    swapped = jnp.concatenate([coeffs[..., channels:], -coeffs[..., :channels]], -1)
    first_half = jnp.einsum(
        "kmp,kmcp->kmc", coeffs, weights_local, preferred_element_type=jnp.float32
    )
    second_half = jnp.einsum(
        "kmp,kmcp->kmc", swapped, weights_local, preferred_element_type=jnp.float32
    )
    return jnp.concatenate([first_half, second_half], -1).astype(jnp.bfloat16)


def pointwise(local_field, weights_small):
    planes, y_count, last_width = local_field.shape
    channels = weights_small.shape[0]
    paired = jnp.kron(jnp.eye(2, dtype=weights_small.dtype), weights_small)
    cell_pairs = local_field.reshape(planes * y_count * last_width // (2 * channels), 2 * channels)
    return jnp.dot(cell_pairs, paired, preferred_element_type=jnp.float32).reshape(
        planes, y_count, last_width
    )


def sample_sum(left_side, right_side):
    channels = left_side.shape[-1] // 2
    left_real = left_side[..., :channels]
    left_imag = left_side[..., channels:]
    right_real = right_side[..., :channels]
    right_imag = right_side[..., channels:]

    def outer_sum(left_op, right_op):
        return jnp.einsum("skmc,skmo->kmco", left_op, right_op, preferred_element_type=jnp.float32)

    real_sum = outer_sum(left_real, right_real) + outer_sum(left_imag, right_imag)
    imag_sum = outer_sum(left_real, right_imag) - outer_sum(left_imag, right_real)
    return jnp.concatenate([real_sum, imag_sum], -1)


def partner_rounds(slot_buffer):
    slot_count = slot_buffer.shape[0]
    my_index = lax.axis_index("gx")
    for bit_pos in range(slot_count.bit_length() - 1):
        shaped = slot_buffer.reshape(
            (slot_count >> bit_pos + 1, 2, 1 << bit_pos) + slot_buffer.shape[1:]
        )
        lower_half = shaped[:, 0]
        upper_half = shaped[:, 1]
        own_bit = jnp.bitwise_and(jnp.right_shift(my_index, bit_pos), 1) == 1
        outgoing = jnp.where(own_bit, lower_half, upper_half)
        incoming = partner(outgoing, "gx", bit_pos)
        new_lower = jnp.where(own_bit, incoming, lower_half)
        new_upper = jnp.where(own_bit, upper_half, incoming)
        slot_buffer = jnp.stack([new_lower, new_upper], 1).reshape(slot_buffer.shape)
    return slot_buffer


def toward_modes(mode_data):
    planes, mode_total, pair_width = mode_data.shape
    group_size = lax.axis_size("gx")
    slot_buffer = mode_data.reshape(
        planes, group_size, mode_total // group_size, pair_width
    ).transpose(1, 0, 2, 3)
    return partner_rounds(slot_buffer).reshape(
        planes * group_size, mode_total // group_size, pair_width
    )


def toward_planes(back_planes):
    x_length, mode_block, pair_width = back_planes.shape
    group_size = lax.axis_size("gx")
    slot_buffer = back_planes.reshape(group_size, x_length // group_size, mode_block, pair_width)
    arrived = partner_rounds(slot_buffer)
    return arrived.transpose(1, 0, 2, 3).reshape(
        x_length // group_size, group_size * mode_block, pair_width
    )


MESH = pl.DeviceIdType.MESH
NT = (((1,), (1,)), ((), ()))


def angles_host(freq_count, grid_count):
    frequency = np.arange(freq_count) - freq_count // 2
    turn_index = np.mod(frequency[:, None] * np.arange(grid_count)[None, :], grid_count)
    return turn_index.astype(np.float32) * np.float32(2.0 * math.pi / grid_count)


def host_tables(y_count, z_count, channels):
    theta_y = angles_host(KY, y_count)
    table_y = np.concatenate([np.cos(theta_y), -np.sin(theta_y)], 0)
    theta_z = angles_host(KZ, z_count)
    eye = np.eye(16, dtype=np.float32)
    fwd_z = np.concatenate([np.kron(eye, np.cos(theta_z)), np.kron(eye, np.sin(theta_z))], 0)
    inv_z = np.concatenate([np.kron(eye, np.cos(theta_z).T), np.kron(eye, np.sin(theta_z).T)], 0)
    spread = np.tile(np.eye(channels, dtype=np.float32), (256 // channels, 1))
    return [jnp.asarray(t, jnp.bfloat16) for t in (table_y, table_y.T, fwd_z, inv_z, spread)]


def x_tables(kx_count, x_length):
    theta_x = angles_host(kx_count, x_length)[:x_length]
    rounded = [np.asarray(f(theta_x), jnp.bfloat16).astype(np.float32) for f in (np.cos, np.sin)]
    return [np.where(np.abs(t) < 1e-5, 0.0, t) for t in rounded]


def dot32(left, right):
    return jnp.dot(left, right, preferred_element_type=jnp.float32)


def lanes_low(shape):
    return lax.broadcasted_iota(jnp.int32, shape, 1) < 64


def swap(block):
    return pltpu.roll(block, 64, 1)


def turned(block):
    swapped = swap(block)
    return jnp.where(lanes_low(block.shape), swapped, -swapped)


def x_pass(read, write, cos_t, sin_t, mode_block):
    length = cos_t.shape[0]
    half = length // 2

    def step(index, carry):
        rows = pl.ds(pl.multiple_of(index * 16, 16), 16)
        data = [read(j, rows) for j in range(length)]
        folded = [
            [data[j] + data[j + half] for j in range(half)],
            [data[j] - data[j + half] for j in range(half)],
        ]
        spun = [[turned(block) for block in group] for group in folded]
        for k in range(length):
            total = None
            for j in range(half):
                for coef, block in ((cos_t[k, j], folded[k % 2][j]), (sin_t[k, j], spun[k % 2][j])):
                    coef = float(coef)
                    if coef == 0.0:
                        continue
                    term = block if coef == 1.0 else -block if coef == -1.0 else block * coef
                    total = term if total is None else total + term
            write(k, rows, total)
        return carry

    lax.fori_loop(0, mode_block // 16, step, 0)


def forward_planes(source, table_y, fwd_z, mid, send):
    first_pass = dot32(table_y[...], source[...])
    low = lanes_low((KY, 128))
    for pair in range(first_pass.shape[1] // 128):
        real_in = first_pass[:KY, pair * 128 : pair * 128 + 128]
        imag_in = first_pass[KY:, pair * 128 : pair * 128 + 128]
        mid[:, 2 * pair, :] = jnp.where(low, real_in, swap(imag_in))
        mid[:, 2 * pair + 1, :] = jnp.where(low, swap(real_in), imag_in)
    group_size, mode_block, pair_width = send.shape
    per_half = 256 // mode_block
    for half in range(2):
        block = mid[16 * half : 16 * half + 16].reshape(256, pair_width).astype(jnp.bfloat16)
        both = dot32(fwd_z[...], block)
        data = both[:256] + turned(both[256:])
        send[half * per_half : (half + 1) * per_half] = data.reshape(
            per_half, mode_block, pair_width
        ).astype(jnp.bfloat16)


def inverse_planes(arrived, inv_z, mid, stacked, norm_scale):
    group_size, mode_block, pair_width = arrived.shape
    per_half = 256 // mode_block
    for half in range(2):
        block = arrived[half * per_half : (half + 1) * per_half].reshape(256, pair_width)
        both = dot32(inv_z[...], block)
        mid[16 * half : 16 * half + 16] = (
            (both[:256] - turned(both[256:])) * norm_scale
        ).reshape(16, 16, pair_width)
    low = lanes_low((KY, 128))
    for pair in range(stacked.shape[1] // 128):
        even = mid[:, 2 * pair, :]
        odd = mid[:, 2 * pair + 1, :]
        columns = slice(pair * 128, pair * 128 + 128)
        stacked[:KY, columns] = jnp.where(low, even, swap(odd)).astype(jnp.bfloat16)
        stacked[KY:, columns] = jnp.where(low, swap(even), odd).astype(jnp.bfloat16)


def fused_kernel(
    cos_x, sin_x, norm_scale, group_size, sample_count, alias_count,
    field_hbm, cot_hbm, weights_hbm, point_ref, table_y, table_y_t, fwd_z, inv_z, spread,
    field_out, field_grad, shared_in, shared_grad,
    field, cot, weights, send, arrive, coef_in, coef_grad, mixed, mid, stacked, accum,
    out_block, grad_block, tail_block, point_wide, point_wide_t,
    load_sem, weight_sem, send_sem, recv_sem, sa_send, sa_recv, own_sem,
):
    me = lax.axis_index("gx")
    mine = lax.axis_index("sa")
    x_length = group_size
    mode_block = send.shape[2]
    groups = mode_block // 16

    load_field = pltpu.make_async_copy(field_hbm.at[0, 0], field, load_sem.at[0])
    load_cot = pltpu.make_async_copy(cot_hbm.at[0, 0], cot, load_sem.at[1])
    load_field.start()
    load_cot.start()

    def weight_copy(kx):
        return pltpu.make_async_copy(weights_hbm.at[kx], weights.at[kx], weight_sem.at[kx])

    for residue in range(x_length):
        for alias in range(alias_count):
            weight_copy(residue + x_length * alias).start()

    barrier = pltpu.get_barrier_semaphore()
    for hop in range(1, group_size):
        pl.semaphore_signal(
            barrier, inc=1, device_id={"gx": lax.rem(me + hop, group_size)}, device_id_type=MESH
        )
    for hop in range(1, sample_count):
        pl.semaphore_signal(
            barrier, inc=1, device_id={"sa": lax.rem(mine + hop, sample_count)}, device_id_type=MESH
        )

    def plane_copy(turn, hop):
        target = lax.rem(me + hop, group_size)
        return pltpu.make_async_remote_copy(
            src_ref=send.at[turn, target],
            dst_ref=arrive.at[turn, me],
            send_sem=send_sem.at[turn, hop],
            recv_sem=recv_sem.at[turn, hop],
            device_id={"gx": target},
            device_id_type=MESH,
        )

    def exchange_start(turn):
        for hop in range(1, group_size):
            plane_copy(turn, hop).start()
        arrive[turn, me] = send[turn, me]

    def exchange_wait(turn):
        for hop in range(1, group_size):
            plane_copy(turn, hop).wait_recv()

    def sample_copy(which, hop):
        source, target = ((coef_in, shared_in), (coef_grad, shared_grad))[which]
        return pltpu.make_async_remote_copy(
            src_ref=source,
            dst_ref=target.at[mine],
            send_sem=sa_send.at[which, hop],
            recv_sem=sa_recv.at[which, hop],
            device_id={"sa": lax.rem(mine + hop, sample_count)},
            device_id_type=MESH,
        )

    def own_copy(which):
        source, target = ((coef_in, shared_in), (coef_grad, shared_grad))[which]
        return pltpu.make_async_copy(source, target.at[mine], own_sem.at[which])

    def samples_start(which):
        for hop in range(1, sample_count):
            sample_copy(which, hop).start()
        own_copy(which).start()

    def forward_modes(turn, coef):
        def read(j, rows):
            return arrive[turn, j, rows, :].astype(jnp.float32)

        def write(k, rows, value):
            coef[k, rows, :] = (value * norm_scale).astype(jnp.bfloat16)

        x_pass(read, write, cos_x, sin_x, mode_block)

    def inverse_modes(turn):
        def read(j, rows):
            return mixed[j, rows, :]

        def write(k, rows, value):
            send[turn, k, rows, :] = value.astype(jnp.bfloat16)

        x_pass(read, write, cos_x.T, -sin_x.T, mode_block)

    def fold_weights(residue, carry):
        for alias in range(alias_count):
            weight_copy(residue + x_length * alias).wait()

        def step(index, inner):
            rows = pl.ds(pl.multiple_of(index * 128, 128), 128)
            total = weights[residue, rows, :].astype(jnp.float32)
            for alias in range(1, alias_count):
                total = total + weights[residue + x_length * alias, rows, :].astype(jnp.float32)
            weights[residue, rows, :] = total.astype(jnp.bfloat16)
            return inner

        lax.fori_loop(0, weights.shape[1] // 128, step, 0, unroll=4)
        return carry

    own_lanes = (
        lax.broadcasted_iota(jnp.int32, (16, 1024), 1) // 64
        == lax.broadcasted_iota(jnp.int32, (16, 1024), 0)
    )
    low16 = lanes_low((16, 128))

    def diagonal(block):
        wide = jnp.concatenate([block] * 8, axis=1)
        return jnp.where(own_lanes, wide, 0.0).astype(jnp.bfloat16)

    def gathered(block):
        kept = jnp.where(own_lanes, block, 0.0)
        total = kept[:, :128]
        for part in range(1, 8):
            total = total + kept[:, part * 128 : part * 128 + 128]
        return total + swap(total)

    def mix_in(residue, carry):
        def step(index, inner):
            rows = pl.ds(pl.multiple_of(index * 16, 16), 16)
            coef = coef_in[residue, rows, :].astype(jnp.float32)
            other = swap(coef)
            left = jnp.concatenate(
                [diagonal(jnp.where(low16, coef, other)), diagonal(jnp.where(low16, other, coef))], 0
            )
            right = weights[residue, pl.ds(pl.multiple_of(index * 1024, 1024), 1024), :]
            product = dot32(left, right)
            mixed[residue, rows, :] = product[:16] - turned(product[16:])
            return inner

        lax.fori_loop(0, groups, step, 0, unroll=2)
        return carry

    def mix_back(residue, carry):
        def step(index, inner):
            rows = pl.ds(pl.multiple_of(index * 16, 16), 16)
            coef = coef_grad[residue, rows, :].astype(jnp.float32)
            left = jnp.concatenate([coef, turned(coef)], 0).astype(jnp.bfloat16)
            right = weights[residue, pl.ds(pl.multiple_of(index * 1024, 1024), 1024), :]
            product = lax.dot_general(left, right, NT, preferred_element_type=jnp.float32)
            mixed[residue, rows, :] = jnp.where(low16, gathered(product[:16]), gathered(product[16:]))
            return inner

        lax.fori_loop(0, groups, step, 0, unroll=2)
        return carry

    def pointwise_into(source, wide):
        for part in range(accum.shape[1] // 256):
            columns = slice(part * 256, part * 256 + 256)
            accum[:, columns] = dot32(source[:, columns], wide[...])

    def add_spectrum():
        for part in range(accum.shape[1] // 256):
            columns = slice(part * 256, part * 256 + 256)
            accum[:, columns] += dot32(table_y_t[...], stacked[:, columns])

    load_field.wait()
    forward_planes(field, table_y, fwd_z, mid, send.at[0])
    pl.semaphore_wait(barrier, group_size + sample_count - 2)
    exchange_start(0)

    same_block = (
        lax.broadcasted_iota(jnp.int32, (256, 256), 0) // 64
        == lax.broadcasted_iota(jnp.int32, (256, 256), 1) // 64
    )

    def widened(block):
        wide = lax.dot_general(block.astype(jnp.bfloat16), spread[...], NT, preferred_element_type=jnp.float32)
        return jnp.where(same_block, wide, 0.0).astype(jnp.bfloat16)

    point_wide[...] = widened(dot32(spread[...], point_ref[...]))
    point_wide_t[...] = widened(
        lax.dot_general(spread[...], point_ref[...], NT, preferred_element_type=jnp.float32)
    )
    pointwise_into(field, point_wide)

    early = x_length // 4
    lax.fori_loop(0, early, fold_weights, 0)
    exchange_wait(0)
    forward_modes(0, coef_in)
    samples_start(0)
    lax.fori_loop(0, early, mix_in, 0)
    lax.fori_loop(early, x_length, lambda r, c: mix_in(r, fold_weights(r, c)), 0)
    inverse_modes(1)
    exchange_start(1)
    load_cot.wait()
    exchange_wait(1)
    inverse_planes(arrive.at[1], inv_z, mid, stacked, norm_scale)
    add_spectrum()

    def activate(index, carry):
        rows = pl.ds(pl.multiple_of(index * 16, 16), 16)
        activated, gelu_slope = gelu_parts(accum[rows, :])
        out_block[rows, :] = activated.astype(jnp.bfloat16)
        grad_block[rows, :] = (cot[rows, :].astype(jnp.float32) * gelu_slope).astype(jnp.bfloat16)
        return carry

    lax.fori_loop(0, accum.shape[0] // 16, activate, 0)
    store_out = pltpu.make_async_copy(out_block, field_out.at[0, 0], load_sem.at[2])
    store_out.start()

    forward_planes(grad_block, table_y, fwd_z, mid, send.at[2])
    exchange_start(2)
    pointwise_into(grad_block, point_wide_t)
    exchange_wait(2)
    forward_modes(2, coef_grad)
    samples_start(1)
    lax.fori_loop(0, x_length, mix_back, 0)
    inverse_modes(3)
    exchange_start(3)
    exchange_wait(3)
    inverse_planes(arrive.at[3], inv_z, mid, stacked, norm_scale)
    add_spectrum()
    tail_block[...] = accum[...].astype(jnp.bfloat16)
    store_grad = pltpu.make_async_copy(tail_block, field_grad.at[0, 0], load_sem.at[3])
    store_grad.start()

    for turn in range(4):
        for hop in range(1, group_size):
            plane_copy(turn, hop).wait_send()
    for which in range(2):
        own_copy(which).wait()
        for hop in range(1, sample_count):
            sample_copy(which, hop).wait()
    store_out.wait()
    store_grad.wait()


def weight_kernel(left_ref, right_ref, out_ref):
    sample_count = left_ref.shape[0]
    depth = 2 * sample_count * 16
    own_lane = lax.broadcasted_iota(jnp.int32, (64, depth), 1) % 16
    for group in range(left_ref.shape[2] // 16):
        rows = slice(group * 16, group * 16 + 16)
        left = jnp.concatenate([left_ref[s, 0, rows, :] for s in range(sample_count)], 0)
        right = jnp.concatenate([right_ref[s, 0, rows, :] for s in range(sample_count)], 0)
        flipped = left.astype(jnp.float32).T
        flipped = jnp.concatenate([flipped[:64], flipped[64:]], axis=1)
        wide = right.astype(jnp.float32)
        stack = jnp.concatenate([wide, turned(wide)], 0).astype(jnp.bfloat16)
        for mode in range(16):
            kept = jnp.where(own_lane == mode, flipped, 0.0).astype(jnp.bfloat16)
            out_ref[0, group * 16 + mode] = dot32(kept, stack)


def fused_device(field_in, cotangent, mode_weights, point_weights):
    y_count, last_width = field_in.shape[2:]
    channels = point_weights.shape[0]
    z_count = last_width // channels
    kx_count, mode_block = mode_weights.shape[:2]
    group_size = lax.axis_size("gx")
    sample_count = lax.axis_size("sa")
    x_length = group_size
    pair_width = 2 * channels
    norm_scale = 1.0 / math.sqrt(x_length * y_count * z_count)
    cos_x, sin_x = x_tables(kx_count, x_length)
    bf16, f32 = jnp.bfloat16, jnp.float32
    plane = (y_count, last_width)
    coef_shape = (x_length, mode_block, pair_width)
    anywhere = pl.BlockSpec(memory_space=pl.ANY)
    vmem = pl.BlockSpec(memory_space=pltpu.VMEM)
    field_out, field_grad, shared_in, shared_grad = pl.pallas_call(
        functools.partial(
            fused_kernel, cos_x, sin_x, norm_scale, group_size, sample_count, kx_count // x_length
        ),
        out_shape=[
            jax.ShapeDtypeStruct((1, 1) + plane, bf16),
            jax.ShapeDtypeStruct((1, 1) + plane, bf16),
            jax.ShapeDtypeStruct((sample_count,) + coef_shape, bf16),
            jax.ShapeDtypeStruct((sample_count,) + coef_shape, bf16),
        ],
        in_specs=[anywhere] * 3 + [vmem] * 6,
        out_specs=[anywhere] * 4,
        scratch_shapes=[
            pltpu.VMEM(plane, bf16),
            pltpu.VMEM(plane, bf16),
            pltpu.VMEM((kx_count, mode_block * channels, pair_width), bf16),
            pltpu.VMEM((4,) + coef_shape, bf16),
            pltpu.VMEM((4,) + coef_shape, bf16),
            pltpu.VMEM(coef_shape, bf16),
            pltpu.VMEM(coef_shape, bf16),
            pltpu.VMEM(coef_shape, f32),
            pltpu.VMEM((KY, z_count, pair_width), f32),
            pltpu.VMEM((2 * KY, last_width), bf16),
            pltpu.VMEM(plane, f32),
            pltpu.VMEM(plane, bf16),
            pltpu.VMEM(plane, bf16),
            pltpu.VMEM(plane, bf16),
            pltpu.VMEM((256, 256), bf16),
            pltpu.VMEM((256, 256), bf16),
            pltpu.SemaphoreType.DMA((4,)),
            pltpu.SemaphoreType.DMA((kx_count,)),
            pltpu.SemaphoreType.DMA((4, group_size)),
            pltpu.SemaphoreType.DMA((4, group_size)),
            pltpu.SemaphoreType.DMA((2, sample_count)),
            pltpu.SemaphoreType.DMA((2, sample_count)),
            pltpu.SemaphoreType.DMA((2,)),
        ],
        compiler_params=pltpu.CompilerParams(
            collective_id=0, has_side_effects=True, vmem_limit_bytes=56 * 1024 * 1024
        ),
        name="fourier_layer",
    )(
        field_in, cotangent,
        mode_weights.reshape(kx_count, mode_block * channels, pair_width),
        point_weights, *host_tables(y_count, z_count, channels),
    )
    coef_spec = pl.BlockSpec((sample_count, 1, mode_block, pair_width), lambda r: (0, r, 0, 0))
    weight_grad = pl.pallas_call(
        weight_kernel,
        out_shape=jax.ShapeDtypeStruct((x_length, mode_block, channels, pair_width), f32),
        grid=(x_length,),
        in_specs=[coef_spec, coef_spec],
        out_specs=pl.BlockSpec((1, mode_block, channels, pair_width), lambda r: (r, 0, 0, 0)),
        compiler_params=pltpu.CompilerParams(vmem_limit_bytes=32 * 1024 * 1024),
        name="weight_gradient",
    )(shared_in, shared_grad)
    return field_out, field_grad, weight_grad


def folds(field_in, mode_weights, point_weights):
    group_size, sample_count = lax.axis_size("gx"), lax.axis_size("sa")
    kx_count, mode_block, channels = mode_weights.shape[:3]
    planes, y_count, last_width = field_in.shape[1:]
    return (
        planes == 1
        and field_in.shape[0] == 1
        and channels == 64
        and last_width == 16 * channels
        and y_count % 16 == 0
        and mode_block % 16 == 0
        and 256 % mode_block == 0
        and group_size % 4 == 0
        and kx_count % group_size == 0
        and kx_count == sample_count * group_size
    )


def on_device(field_in, cotangent, mode_weights, point_weights):
    if folds(field_in, mode_weights, point_weights):
        return fused_device(field_in, cotangent, mode_weights, point_weights)
    local_field = field_in[0]
    planes, y_count, last_width = local_field.shape
    channels = point_weights.shape[0]
    z_count = last_width // channels
    kx_count = mode_weights.shape[0]
    x_length = planes * lax.axis_size("gx")
    norm_scale = 1.0 / math.sqrt(x_length * y_count * z_count)
    coeffs_in = forward_x(toward_modes(forward_yz(local_field, channels)), kx_count, norm_scale)
    mixed_modes = mix_forward(coeffs_in, mode_weights)
    spec_out = inverse_yz(
        toward_planes(inverse_x(mixed_modes, x_length)), y_count, z_count, norm_scale
    )
    pre_act = spec_out + pointwise(local_field, point_weights)
    activated, gelu_slope = gelu_parts(pre_act)
    out_grad = (cotangent[0].astype(jnp.float32) * gelu_slope).astype(jnp.bfloat16)
    coeffs_grad = forward_x(toward_modes(forward_yz(out_grad, channels)), kx_count, norm_scale)
    back_modes = mix_backward(coeffs_grad, mode_weights)
    spec_grad = inverse_yz(
        toward_planes(inverse_x(back_modes, x_length)), y_count, z_count, norm_scale
    )
    field_grad = (spec_grad + pointwise(out_grad, point_weights.T)).astype(jnp.bfloat16)
    shared_in, shared_grad = (
        lax.all_to_all(coeffs_in[None], "sa", split_axis=1, concat_axis=0, tiled=True),
        lax.all_to_all(coeffs_grad[None], "sa", split_axis=1, concat_axis=0, tiled=True),
    )
    weight_grad = sample_sum(shared_in, shared_grad)
    return (activated.astype(jnp.bfloat16)[None], field_grad[None], weight_grad)


def solution(mesh):
    in_specs = (
        P("sa", "gx", None, None),
        P("sa", "gx", None, None),
        P(None, "gx", None, None),
        P(),
    )
    out_specs = (P("sa", "gx", None, None), P("sa", "gx", None, None), P("sa", "gx", None, None))
    return jax.shard_map(
        on_device, mesh=mesh, in_specs=in_specs, out_specs=out_specs, check_vma=False
    )
```

profile of v0, /device:TPU:0, one launch (start us, length us, event | category | flops | bytes accessed | tf_op | source)
XLA Modules:
  0.0 66.8 jit_solution(11282667445766870742)
XLA Ops:
  0.6 50.8 %fourier_layer.1 = (bf16[1,1,256,1024]{3,2,1,0:T(8,128)(2,1)}, bf16[1,1,256,1024]{3,2,1,0:T(8,128)(2,1)}, bf16[4,8,64,128]{3,2,1,0:T(8,128)(2,1)}, bf16[4,8,64,128]{3,2,1,0:T(8,128)(2,1)}) custom-call(bf16[1,1,256,1024]{3,2,1,0:T(8,128)(2,1)} %field_hbm.1, bf16[1,1,256,1024]{3,2,1,0:T(8,128)(2,1)} %cot_hbm.1, bf16[32,4096,128]{2,1,0:T(8,128)(2,1)} %bitcast.1, ...), custom_call_target="tpu_custom_call" | custom-call | tf_op jit(solution)/shard_map/fourier_layer/pallas_call | solution.py:590
  51.5 0.0 copy-start
  51.5 1.0 %copy-done = bf16[4,8,64,128]{3,2,1,0:T(8,128)(2,1)S(1)} copy-done((bf16[4,8,64,128]{3,2,1,0:T(8,128)(2,1)S(1)}, bf16[4,8,64,128]{3,2,1,0:T(8,128)(2,1)}, u32[]{:S(2)}) %copy-start) | copy-done | bytes 524312
  52.5 0.0 copy-start.1
  52.5 1.0 %copy-done.1 = bf16[4,8,64,128]{3,2,1,0:T(8,128)(2,1)S(1)} copy-done((bf16[4,8,64,128]{3,2,1,0:T(8,128)(2,1)S(1)}, bf16[4,8,64,128]{3,2,1,0:T(8,128)(2,1)}, u32[]{:S(2)}) %copy-start.1) | copy-done | bytes 524312
  53.6 9.5 %weight_gradient.1 = f32[8,64,64,128]{3,2,1,0:T(8,128)} custom-call(bf16[4,8,64,128]{3,2,1,0:T(8,128)(2,1)S(1)} %copy-done, bf16[4,8,64,128]{3,2,1,0:T(8,128)(2,1)S(1)} %copy-done.1), custom_call_target="tpu_custom_call" | custom-call | tf_op jit(solution)/shard_map/weight_gradient/pallas_call | solution.py:637
  63.1 1.9 %copy.14 = bf16[1,1,256,1024]{3,2,1,0:T(8,128)(2,1)} copy(bf16[1,1,256,1024]{3,2,1,0:T(8,128)(2,1)} %get-tuple-element.14) | data formatting | bytes 1048576
  65.0 1.9 %copy.15 = bf16[1,1,256,1024]{3,2,1,0:T(8,128)(2,1)} copy(bf16[1,1,256,1024]{3,2,1,0:T(8,128)(2,1)} %get-tuple-element.15) | data formatting | bytes 1048576
Async XLA Ops:
  51.5 1.0 %copy-start = (bf16[4,8,64,128]{3,2,1,0:T(8,128)(2,1)S(1)}, bf16[4,8,64,128]{3,2,1,0:T(8,128)(2,1)}, u32[]{:S(2)}) copy-start(bf16[4,8,64,128]{3,2,1,0:T(8,128)(2,1)} %get-tuple-element.9.left_ref) | copy-start | bytes 1572868
  52.5 1.0 %copy-start.1 = (bf16[4,8,64,128]{3,2,1,0:T(8,128)(2,1)S(1)}, bf16[4,8,64,128]{3,2,1,0:T(8,128)(2,1)}, u32[]{:S(2)}) copy-start(bf16[4,8,64,128]{3,2,1,0:T(8,128)(2,1)} %get-tuple-element.10.right_ref) | copy-start | bytes 1572868
where the time goes:
time: 67.1 us; the launch traced here: 66.8 us
  Pallas kernels  60.4 us (90%)
  local copies, waits for them, and re-layouts  5.81 us (9%)
    pallas_call x1, Pallas kernels, fused_device(): pl.pallas_call(functools.partial(fused_kernel, cos_x, sin_x, norm_scale,...  50.8 us
    pallas_call x1, Pallas kernels, fused_device(): pl.pallas_call(weight_kernel, out_shape=jax.ShapeDtypeStruct((x_length, m...  9.52 us
    unnamed x6, local copies, waits for them, and re-layouts  5.81 us

commit v1 on v0

--- a/solution.py
+++ b/solution.py
@@ -211,6 +211,7 @@
 
 MESH = pl.DeviceIdType.MESH
 NT = (((1,), (1,)), ((), ()))
+ROOT_CONST = math.sqrt(2.0 / math.pi)
 
 
 def angles_host(freq_count, grid_count):
@@ -321,7 +322,7 @@
     cos_x, sin_x, norm_scale, group_size, sample_count, alias_count,
     field_hbm, cot_hbm, weights_hbm, point_ref, table_y, table_y_t, fwd_z, inv_z, spread,
     field_out, field_grad, shared_in, shared_grad,
-    field, cot, weights, send, arrive, coef_in, coef_grad, mixed, mid, stacked, accum,
+    field, cot, weights, folded, send, arrive, coef_in, coef_grad, mixed, mid, stacked, accum,
     out_block, grad_block, tail_block, point_wide, point_wide_t,
     load_sem, weight_sem, send_sem, recv_sem, sa_send, sa_recv, own_sem,
 ):
@@ -411,19 +412,26 @@
 
         x_pass(read, write, cos_x.T, -sin_x.T, mode_block)
 
-    def fold_weights(residue, carry):
+    def wait_weights(residue):
         for alias in range(alias_count):
             weight_copy(residue + x_length * alias).wait()
 
-        def step(index, inner):
-            rows = pl.ds(pl.multiple_of(index * 128, 128), 128)
+    def fold_rows(residue, start, count):
+        for part in range(count // 128):
+            rows = pl.ds(pl.multiple_of(start + part * 128, 128), 128)
             total = weights[residue, rows, :].astype(jnp.float32)
             for alias in range(1, alias_count):
                 total = total + weights[residue + x_length * alias, rows, :].astype(jnp.float32)
-            weights[residue, rows, :] = total.astype(jnp.bfloat16)
+            folded[residue, rows, :] = total.astype(jnp.bfloat16)
+
+    def fold_weights(residue, carry):
+        wait_weights(residue)
+
+        def step(index, inner):
+            fold_rows(residue, index * 1024, 1024)
             return inner
 
-        lax.fori_loop(0, weights.shape[1] // 128, step, 0, unroll=4)
+        lax.fori_loop(0, groups, step, 0)
         return carry
 
     own_lanes = (
@@ -443,33 +451,38 @@
             total = total + kept[:, part * 128 : part * 128 + 128]
         return total + swap(total)
 
+    def mix_in_group(residue, group):
+        rows = slice(group * 16, group * 16 + 16)
+        coef = coef_in[residue, rows, :].astype(jnp.float32)
+        other = swap(coef)
+        left = jnp.concatenate(
+            [diagonal(jnp.where(low16, coef, other)), diagonal(jnp.where(low16, other, coef))], 0
+        )
+        product = dot32(left, folded[residue, group * 1024 : group * 1024 + 1024, :])
+        mixed[residue, rows, :] = product[:16] - turned(product[16:])
+
     def mix_in(residue, carry):
-        def step(index, inner):
-            rows = pl.ds(pl.multiple_of(index * 16, 16), 16)
-            coef = coef_in[residue, rows, :].astype(jnp.float32)
-            other = swap(coef)
-            left = jnp.concatenate(
-                [diagonal(jnp.where(low16, coef, other)), diagonal(jnp.where(low16, other, coef))], 0
-            )
-            right = weights[residue, pl.ds(pl.multiple_of(index * 1024, 1024), 1024), :]
-            product = dot32(left, right)
-            mixed[residue, rows, :] = product[:16] - turned(product[16:])
-            return inner
-
-        lax.fori_loop(0, groups, step, 0, unroll=2)
+        for group in range(groups):
+            mix_in_group(residue, group)
         return carry
 
+    def mix_and_fold(residue, carry):
+        wait_weights(residue)
+        for group in range(groups):
+            mix_in_group(residue - 1, group)
+            fold_rows(residue, group * 1024, 1024)
+        return carry
+
     def mix_back(residue, carry):
-        def step(index, inner):
-            rows = pl.ds(pl.multiple_of(index * 16, 16), 16)
+        for group in range(groups):
+            rows = slice(group * 16, group * 16 + 16)
             coef = coef_grad[residue, rows, :].astype(jnp.float32)
             left = jnp.concatenate([coef, turned(coef)], 0).astype(jnp.bfloat16)
-            right = weights[residue, pl.ds(pl.multiple_of(index * 1024, 1024), 1024), :]
+            right = folded[residue, group * 1024 : group * 1024 + 1024, :]
             product = lax.dot_general(left, right, NT, preferred_element_type=jnp.float32)
-            mixed[residue, rows, :] = jnp.where(low16, gathered(product[:16]), gathered(product[16:]))
-            return inner
-
-        lax.fori_loop(0, groups, step, 0, unroll=2)
+            mixed[residue, rows, :] = jnp.where(
+                low16, gathered(product[:16]), gathered(product[16:])
+            )
         return carry
 
     def pointwise_into(source, wide):
@@ -502,13 +515,14 @@
     )
     pointwise_into(field, point_wide)
 
-    early = x_length // 4
+    early = 3
     lax.fori_loop(0, early, fold_weights, 0)
     exchange_wait(0)
     forward_modes(0, coef_in)
     samples_start(0)
-    lax.fori_loop(0, early, mix_in, 0)
-    lax.fori_loop(early, x_length, lambda r, c: mix_in(r, fold_weights(r, c)), 0)
+    lax.fori_loop(0, early - 1, mix_in, 0)
+    lax.fori_loop(early, x_length, mix_and_fold, 0)
+    mix_in(x_length - 1, 0)
     inverse_modes(1)
     exchange_start(1)
     load_cot.wait()
@@ -518,7 +532,12 @@
 
     def activate(index, carry):
         rows = pl.ds(pl.multiple_of(index * 16, 16), 16)
-        activated, gelu_slope = gelu_parts(accum[rows, :])
+        pre_act = accum[rows, :]
+        square = pre_act * pre_act
+        half_gate = 0.5 + 0.5 * jnp.tanh(pre_act * (ROOT_CONST + ROOT_CONST * GELU_COEF * square))
+        activated = pre_act * half_gate
+        inner_slope = 2.0 * ROOT_CONST + 6.0 * ROOT_CONST * GELU_COEF * square
+        gelu_slope = half_gate + activated * (1.0 - half_gate) * inner_slope
         out_block[rows, :] = activated.astype(jnp.bfloat16)
         grad_block[rows, :] = (cot[rows, :].astype(jnp.float32) * gelu_slope).astype(jnp.bfloat16)
         return carry
@@ -533,7 +552,7 @@
     exchange_wait(2)
     forward_modes(2, coef_grad)
     samples_start(1)
-    lax.fori_loop(0, x_length, mix_back, 0)
+    lax.fori_loop(0, x_length, mix_back, 0, unroll=2)
     inverse_modes(3)
     exchange_start(3)
     exchange_wait(3)
@@ -554,21 +573,56 @@
     store_grad.wait()
 
 
-def weight_kernel(left_ref, right_ref, out_ref):
-    sample_count = left_ref.shape[0]
+def weight_kernel(
+    left_hbm, right_hbm, first_hbm, second_hbm, weight_out, first_out, second_out,
+    left_ref, right_ref, blocks, load_sem, pass_sem, block_sem,
+):
+    loads = [
+        pltpu.make_async_copy(left_hbm, left_ref, load_sem.at[0]),
+        pltpu.make_async_copy(right_hbm, right_ref, load_sem.at[1]),
+    ]
+    passes = [
+        pltpu.make_async_copy(first_hbm, first_out, pass_sem.at[0]),
+        pltpu.make_async_copy(second_hbm, second_out, pass_sem.at[1]),
+    ]
+    for copy in loads + passes:
+        copy.start()
+    for copy in loads:
+        copy.wait()
+    sample_count, x_length, mode_block = left_ref.shape[:3]
     depth = 2 * sample_count * 16
+    groups = mode_block // 16
     own_lane = lax.broadcasted_iota(jnp.int32, (64, depth), 1) % 16
-    for group in range(left_ref.shape[2] // 16):
-        rows = slice(group * 16, group * 16 + 16)
-        left = jnp.concatenate([left_ref[s, 0, rows, :] for s in range(sample_count)], 0)
-        right = jnp.concatenate([right_ref[s, 0, rows, :] for s in range(sample_count)], 0)
-        flipped = left.astype(jnp.float32).T
-        flipped = jnp.concatenate([flipped[:64], flipped[64:]], axis=1)
-        wide = right.astype(jnp.float32)
-        stack = jnp.concatenate([wide, turned(wide)], 0).astype(jnp.bfloat16)
-        for mode in range(16):
-            kept = jnp.where(own_lane == mode, flipped, 0.0).astype(jnp.bfloat16)
-            out_ref[0, group * 16 + mode] = dot32(kept, stack)
+
+    def block_copy(index):
+        return pltpu.make_async_copy(blocks.at[index], weight_out.at[index], block_sem.at[index])
+
+    def step(residue, carry):
+        for group in range(groups):
+            index = residue * groups + group
+            rows = slice(group * 16, group * 16 + 16)
+            left = jnp.concatenate([left_ref[s, residue, rows, :] for s in range(sample_count)], 0)
+            right = jnp.concatenate([right_ref[s, residue, rows, :] for s in range(sample_count)], 0)
+            flipped = left.astype(jnp.float32).T
+            flipped = jnp.concatenate([flipped[:64], flipped[64:]], axis=1)
+            wide = right.astype(jnp.float32)
+            stack = jnp.concatenate([wide, turned(wide)], 0).astype(jnp.bfloat16)
+            kept = jnp.concatenate(
+                [jnp.where(own_lane == mode, flipped, 0.0).astype(jnp.bfloat16) for mode in range(16)], 0
+            )
+            blocks[index] = dot32(kept, stack)
+            block_copy(index).start()
+        return carry
+
+    lax.fori_loop(0, x_length, step, 0)
+
+    def finish(index, carry):
+        block_copy(index).wait()
+        return carry
+
+    lax.fori_loop(0, x_length * groups, finish, 0)
+    for copy in passes:
+        copy.wait()
 
 
 def fused_device(field_in, cotangent, mode_weights, point_weights):
@@ -603,6 +657,7 @@
             pltpu.VMEM(plane, bf16),
             pltpu.VMEM(plane, bf16),
             pltpu.VMEM((kx_count, mode_block * channels, pair_width), bf16),
+            pltpu.VMEM((x_length, mode_block * channels, pair_width), bf16),
             pltpu.VMEM((4,) + coef_shape, bf16),
             pltpu.VMEM((4,) + coef_shape, bf16),
             pltpu.VMEM(coef_shape, bf16),
@@ -633,17 +688,31 @@
         mode_weights.reshape(kx_count, mode_block * channels, pair_width),
         point_weights, *host_tables(y_count, z_count, channels),
     )
-    coef_spec = pl.BlockSpec((sample_count, 1, mode_block, pair_width), lambda r: (0, r, 0, 0))
-    weight_grad = pl.pallas_call(
+    groups = mode_block // 16
+    weight_grad, field_out, field_grad = pl.pallas_call(
         weight_kernel,
-        out_shape=jax.ShapeDtypeStruct((x_length, mode_block, channels, pair_width), f32),
-        grid=(x_length,),
-        in_specs=[coef_spec, coef_spec],
-        out_specs=pl.BlockSpec((1, mode_block, channels, pair_width), lambda r: (r, 0, 0, 0)),
-        compiler_params=pltpu.CompilerParams(vmem_limit_bytes=32 * 1024 * 1024),
+        out_shape=[
+            jax.ShapeDtypeStruct((x_length * groups, 16 * channels, pair_width), f32),
+            jax.ShapeDtypeStruct((1, 1) + plane, bf16),
+            jax.ShapeDtypeStruct((1, 1) + plane, bf16),
+        ],
+        in_specs=[anywhere] * 4,
+        out_specs=[anywhere] * 3,
+        scratch_shapes=[
+            pltpu.VMEM((sample_count,) + coef_shape, bf16),
+            pltpu.VMEM((sample_count,) + coef_shape, bf16),
+            pltpu.VMEM((x_length * groups, 16 * channels, pair_width), f32),
+            pltpu.SemaphoreType.DMA((2,)),
+            pltpu.SemaphoreType.DMA((2,)),
+            pltpu.SemaphoreType.DMA((x_length * groups,)),
+        ],
+        compiler_params=pltpu.CompilerParams(vmem_limit_bytes=56 * 1024 * 1024),
         name="weight_gradient",
-    )(shared_in, shared_grad)
-    return field_out, field_grad, weight_grad
+    )(shared_in, shared_grad, field_out, field_grad)
+    return (
+        field_out, field_grad,
+        weight_grad.reshape(x_length, mode_block, channels, pair_width),
+    )
 
 
 def folds(field_in, mode_weights, point_weights):

time: 67.1 us -> 80.7 us (1.20)
  Pallas kernels: 60.4 us -> 79.9 us
  local copies, waits for them, and re-layouts: 5.81 us -> 0 us
    pallas_call x1, Pallas kernels: 9.52 us -> 33.2 us  [fused_device(): pl.pallas_call(weight_kernel, out_shape=[jax.ShapeDtypeStruct((x_length *...]
    unnamed x6 -> x0, local copies, waits for them, and re-layouts: 5.81 us -> none
    pallas_call x1, Pallas kernels: 50.8 us -> 46.7 us  [fused_device(): pl.pallas_call(functools.partial(fused_kernel, cos_x, sin_x, norm_scale,...]
where the time goes in v1:
time: 80.7 us; the launch traced here: 80.5 us
  Pallas kernels  79.9 us (99%)
    pallas_call x1, Pallas kernels, fused_device(): pl.pallas_call(functools.partial(fused_kernel, cos_x, sin_x, norm_scale,...  46.7 us
    pallas_call x1, Pallas kernels, fused_device(): pl.pallas_call(weight_kernel, out_shape=[jax.ShapeDtypeStruct((x_length *...  33.2 us

profile of v1, /device:TPU:0, one launch (start us, length us, event | category | flops | bytes accessed | tf_op | source)
XLA Modules:
  0.0 80.5 jit_solution(11760021178505692693)
XLA Ops:
  0.6 46.7 %fourier_layer.1 = (bf16[1,1,256,1024]{3,2,1,0:T(8,128)(2,1)}, bf16[1,1,256,1024]{3,2,1,0:T(8,128)(2,1)}, bf16[4,8,64,128]{3,2,1,0:T(8,128)(2,1)}, bf16[4,8,64,128]{3,2,1,0:T(8,128)(2,1)}) custom-call(bf16[1,1,256,1024]{3,2,1,0:T(8,128)(2,1)} %field_hbm.1, bf16[1,1,256,1024]{3,2,1,0:T(8,128)(2,1)} %cot_hbm.1, bf16[32,4096,128]{2,1,0:T(8,128)(2,1)} %bitcast.2, ...), custom_call_target="tpu_custom_call" | custom-call | tf_op jit(solution)/shard_map/fourier_layer/pallas_call | solution.py:644
  47.3 33.2 %weight_gradient.1 = (f32[32,1024,128]{2,1,0:T(8,128)}, bf16[1,1,256,1024]{3,2,1,0:T(8,128)(2,1)}, bf16[1,1,256,1024]{3,2,1,0:T(8,128)(2,1)}) custom-call(bf16[4,8,64,128]{3,2,1,0:T(8,128)(2,1)} %get-tuple-element.10.left_hbm, bf16[4,8,64,128]{3,2,1,0:T(8,128)(2,1)} %get-tuple-element.11.right_hbm, bf16[1,1,256,1024]{3,2,1,0:T(8,128)(2,1)} %get-tuple-element.12.first_hbm, ...), custom_call_target="tpu_custom_call" | custom-call | tf_op jit(solution)/shard_map/weight_gradient/pallas_call | solution.py:692

commit v2 on v1

--- a/solution.py
+++ b/solution.py
@@ -416,73 +416,96 @@
         for alias in range(alias_count):
             weight_copy(residue + x_length * alias).wait()
 
-    def fold_rows(residue, start, count):
-        for part in range(count // 128):
+    def fold_rows(pair, start):
+        for part in range(1024 // 128):
             rows = pl.ds(pl.multiple_of(start + part * 128, 128), 128)
-            total = weights[residue, rows, :].astype(jnp.float32)
-            for alias in range(1, alias_count):
-                total = total + weights[residue + x_length * alias, rows, :].astype(jnp.float32)
-            folded[residue, rows, :] = total.astype(jnp.bfloat16)
-
-    def fold_weights(residue, carry):
-        wait_weights(residue)
+            for side in range(2):
+                residue = 2 * pair + side
+                total = weights[residue, rows, :].astype(jnp.float32)
+                for alias in range(1, alias_count):
+                    total = total + weights[residue + x_length * alias, rows, :].astype(jnp.float32)
+                folded[pair, rows, side * 128 : side * 128 + 128] = total.astype(jnp.bfloat16)
+
+    row_index = lax.broadcasted_iota(jnp.int32, (8, 128), 0)
+    low16 = lanes_low((16, 128))
+    own_half = (row_index + lax.broadcasted_iota(jnp.int32, (8, 128), 1) // 64) % 2 == 0
+    own_pair = [row_index // 2 == pair for pair in range(4)]
+
+    def diagonal(block):
+        empty = jnp.zeros((8, 128), jnp.float32)
+        columns = []
+        for part in range(8):
+            half = block[:8] if part < 4 else block[8:]
+            kept = jnp.where(own_pair[part % 4], jnp.where(own_half, half, 0.0), 0.0)
+            stacked_rows = [kept, empty] if part < 4 else [empty, kept]
+            columns.append(jnp.concatenate(stacked_rows, 0).astype(jnp.bfloat16))
+        return jnp.concatenate(columns, 1)
+
+    def gathered(block):
+        halves = []
+        for half in range(2):
+            rows = slice(half * 8, half * 8 + 8)
+            kept = block[rows, half * 512 : half * 512 + 128]
+            for part in range(1, 4):
+                start = half * 512 + part * 128
+                kept = jnp.where(own_pair[part], block[rows, start : start + 128], kept)
+            halves.append(jnp.where(own_half, kept, 0.0))
+        total = jnp.concatenate(halves, 0)
+        return total + swap(total)
+
+    def mix_in_group(pair, group):
+        rows = slice(group * 16, group * 16 + 16)
+        parts = []
+        for side in range(2):
+            coef = coef_in[2 * pair + side, rows, :].astype(jnp.float32)
+            other = swap(coef)
+            parts += [diagonal(jnp.where(low16, coef, other)), diagonal(jnp.where(low16, other, coef))]
+        product = dot32(
+            jnp.concatenate(parts, 0), folded[pair, group * 1024 : group * 1024 + 1024, :]
+        )
+        for side in range(2):
+            own = product[side * 32 : side * 32 + 32, side * 128 : side * 128 + 128]
+            mixed[2 * pair + side, rows, :] = own[:16] - turned(own[16:])
+
+    def wait_pair(pair):
+        wait_weights(2 * pair)
+        wait_weights(2 * pair + 1)
+
+    def fold_first(pair):
+        wait_pair(pair)
 
         def step(index, inner):
-            fold_rows(residue, index * 1024, 1024)
+            fold_rows(pair, index * 1024)
             return inner
 
         lax.fori_loop(0, groups, step, 0)
+
+    def mix_and_fold(pair, carry):
+        wait_pair(pair)
+        for group in range(groups):
+            mix_in_group(pair - 1, group)
+            fold_rows(pair, group * 1024)
         return carry
 
-    own_lanes = (
-        lax.broadcasted_iota(jnp.int32, (16, 1024), 1) // 64
-        == lax.broadcasted_iota(jnp.int32, (16, 1024), 0)
-    )
-    low16 = lanes_low((16, 128))
-
-    def diagonal(block):
-        wide = jnp.concatenate([block] * 8, axis=1)
-        return jnp.where(own_lanes, wide, 0.0).astype(jnp.bfloat16)
-
-    def gathered(block):
-        kept = jnp.where(own_lanes, block, 0.0)
-        total = kept[:, :128]
-        for part in range(1, 8):
-            total = total + kept[:, part * 128 : part * 128 + 128]
-        return total + swap(total)
-
-    def mix_in_group(residue, group):
-        rows = slice(group * 16, group * 16 + 16)
-        coef = coef_in[residue, rows, :].astype(jnp.float32)
-        other = swap(coef)
-        left = jnp.concatenate(
-            [diagonal(jnp.where(low16, coef, other)), diagonal(jnp.where(low16, other, coef))], 0
-        )
-        product = dot32(left, folded[residue, group * 1024 : group * 1024 + 1024, :])
-        mixed[residue, rows, :] = product[:16] - turned(product[16:])
-
-    def mix_in(residue, carry):
-        for group in range(groups):
-            mix_in_group(residue, group)
-        return carry
-
-    def mix_and_fold(residue, carry):
-        wait_weights(residue)
-        for group in range(groups):
-            mix_in_group(residue - 1, group)
-            fold_rows(residue, group * 1024, 1024)
-        return carry
-
-    def mix_back(residue, carry):
+    def mix_back(pair, carry):
+        empty = jnp.zeros((32, 128), jnp.bfloat16)
         for group in range(groups):
             rows = slice(group * 16, group * 16 + 16)
-            coef = coef_grad[residue, rows, :].astype(jnp.float32)
-            left = jnp.concatenate([coef, turned(coef)], 0).astype(jnp.bfloat16)
-            right = folded[residue, group * 1024 : group * 1024 + 1024, :]
-            product = lax.dot_general(left, right, NT, preferred_element_type=jnp.float32)
-            mixed[residue, rows, :] = jnp.where(
-                low16, gathered(product[:16]), gathered(product[16:])
+            parts = []
+            for side in range(2):
+                coef = coef_grad[2 * pair + side, rows, :].astype(jnp.float32)
+                both = jnp.concatenate([coef, turned(coef)], 0).astype(jnp.bfloat16)
+                parts.append(jnp.concatenate([both, empty] if side == 0 else [empty, both], 1))
+            product = lax.dot_general(
+                jnp.concatenate(parts, 0), folded[pair, group * 1024 : group * 1024 + 1024, :],
+                NT, preferred_element_type=jnp.float32,
             )
+            for side in range(2):
+                start = side * 32
+                mixed[2 * pair + side, rows, :] = jnp.where(
+                    low16, gathered(product[start : start + 16]),
+                    gathered(product[start + 16 : start + 32]),
+                )
         return carry
 
     def pointwise_into(source, wide):
@@ -515,14 +538,13 @@
     )
     pointwise_into(field, point_wide)
 
-    early = 3
-    lax.fori_loop(0, early, fold_weights, 0)
+    fold_first(0)
     exchange_wait(0)
     forward_modes(0, coef_in)
     samples_start(0)
-    lax.fori_loop(0, early - 1, mix_in, 0)
-    lax.fori_loop(early, x_length, mix_and_fold, 0)
-    mix_in(x_length - 1, 0)
+    lax.fori_loop(1, x_length // 2, mix_and_fold, 0)
+    for group in range(groups):
+        mix_in_group(x_length // 2 - 1, group)
     inverse_modes(1)
     exchange_start(1)
     load_cot.wait()
@@ -552,7 +574,7 @@
     exchange_wait(2)
     forward_modes(2, coef_grad)
     samples_start(1)
-    lax.fori_loop(0, x_length, mix_back, 0, unroll=2)
+    lax.fori_loop(0, x_length // 2, mix_back, 0)
     inverse_modes(3)
     exchange_start(3)
     exchange_wait(3)
@@ -575,17 +597,21 @@
 
 def weight_kernel(
     left_hbm, right_hbm, first_hbm, second_hbm, weight_out, first_out, second_out,
-    left_ref, right_ref, blocks, load_sem, pass_sem, block_sem,
+    left_ref, right_ref, first_ref, second_ref, blocks, load_sem, pass_sem, block_sem,
 ):
     loads = [
         pltpu.make_async_copy(left_hbm, left_ref, load_sem.at[0]),
         pltpu.make_async_copy(right_hbm, right_ref, load_sem.at[1]),
     ]
+    fetches = [
+        pltpu.make_async_copy(first_hbm, first_ref, load_sem.at[2]),
+        pltpu.make_async_copy(second_hbm, second_ref, load_sem.at[3]),
+    ]
     passes = [
-        pltpu.make_async_copy(first_hbm, first_out, pass_sem.at[0]),
-        pltpu.make_async_copy(second_hbm, second_out, pass_sem.at[1]),
+        pltpu.make_async_copy(first_ref, first_out, pass_sem.at[0]),
+        pltpu.make_async_copy(second_ref, second_out, pass_sem.at[1]),
     ]
-    for copy in loads + passes:
+    for copy in loads + fetches:
         copy.start()
     for copy in loads:
         copy.wait()
@@ -614,7 +640,11 @@
             block_copy(index).start()
         return carry
 
-    lax.fori_loop(0, x_length, step, 0)
+    step(0, 0)
+    for fetch, copy in zip(fetches, passes):
+        fetch.wait()
+        copy.start()
+    lax.fori_loop(1, x_length, step, 0)
 
     def finish(index, carry):
         block_copy(index).wait()
@@ -657,7 +687,7 @@
             pltpu.VMEM(plane, bf16),
             pltpu.VMEM(plane, bf16),
             pltpu.VMEM((kx_count, mode_block * channels, pair_width), bf16),
-            pltpu.VMEM((x_length, mode_block * channels, pair_width), bf16),
+            pltpu.VMEM((x_length // 2, mode_block * channels, 2 * pair_width), bf16),
             pltpu.VMEM((4,) + coef_shape, bf16),
             pltpu.VMEM((4,) + coef_shape, bf16),
             pltpu.VMEM(coef_shape, bf16),
@@ -701,8 +731,10 @@
         scratch_shapes=[
             pltpu.VMEM((sample_count,) + coef_shape, bf16),
             pltpu.VMEM((sample_count,) + coef_shape, bf16),
+            pltpu.VMEM((1, 1) + plane, bf16),
+            pltpu.VMEM((1, 1) + plane, bf16),
             pltpu.VMEM((x_length * groups, 16 * channels, pair_width), f32),
-            pltpu.SemaphoreType.DMA((2,)),
+            pltpu.SemaphoreType.DMA((4,)),
             pltpu.SemaphoreType.DMA((2,)),
             pltpu.SemaphoreType.DMA((x_length * groups,)),
         ],
@@ -725,9 +757,8 @@
         and channels == 64
         and last_width == 16 * channels
         and y_count % 16 == 0
-        and mode_block % 16 == 0
-        and 256 % mode_block == 0
         and group_size % 4 == 0
+        and mode_block == 64
         and kx_count % group_size == 0
         and kx_count == sample_count * group_size
     )

time: 80.7 us -> 55.7 us (0.69)
  Pallas kernels: 79.9 us -> 54.9 us
    pallas_call x1, Pallas kernels: 33.2 us -> 8.07 us  [fused_device(): pl.pallas_call(weight_kernel, out_shape=[jax.ShapeDtypeStruct((x_length *...]
where the time goes in v2:
time: 55.7 us; the launch traced here: 55.5 us
  Pallas kernels  54.9 us (99%)
  between operations  0.64 us (1%)
    pallas_call x1, Pallas kernels, fused_device(): pl.pallas_call(functools.partial(fused_kernel, cos_x, sin_x, norm_scale,...  46.8 us
    pallas_call x1, Pallas kernels, fused_device(): pl.pallas_call(weight_kernel, out_shape=[jax.ShapeDtypeStruct((x_length *...  8.07 us

profile of v2, /device:TPU:0, one launch (start us, length us, event | category | flops | bytes accessed | tf_op | source)
XLA Modules:
  0.0 55.5 jit_solution(9557066354518187745)
XLA Ops:
  0.6 46.8 %fourier_layer.1 = (bf16[1,1,256,1024]{3,2,1,0:T(8,128)(2,1)}, bf16[1,1,256,1024]{3,2,1,0:T(8,128)(2,1)}, bf16[4,8,64,128]{3,2,1,0:T(8,128)(2,1)}, bf16[4,8,64,128]{3,2,1,0:T(8,128)(2,1)}) custom-call(bf16[1,1,256,1024]{3,2,1,0:T(8,128)(2,1)} %field_hbm.1, bf16[1,1,256,1024]{3,2,1,0:T(8,128)(2,1)} %cot_hbm.1, bf16[32,4096,128]{2,1,0:T(8,128)(2,1)} %bitcast.2, ...), custom_call_target="tpu_custom_call" | custom-call | tf_op jit(solution)/shard_map/fourier_layer/pallas_call | solution.py:674
  47.5 8.1 %weight_gradient.1 = (f32[32,1024,128]{2,1,0:T(8,128)}, bf16[1,1,256,1024]{3,2,1,0:T(8,128)(2,1)}, bf16[1,1,256,1024]{3,2,1,0:T(8,128)(2,1)}) custom-call(bf16[4,8,64,128]{3,2,1,0:T(8,128)(2,1)} %get-tuple-element.10.left_hbm, bf16[4,8,64,128]{3,2,1,0:T(8,128)(2,1)} %get-tuple-element.11.right_hbm, bf16[1,1,256,1024]{3,2,1,0:T(8,128)(2,1)} %get-tuple-element.12.first_hbm, ...), custom_call_target="tpu_custom_call" | custom-call | tf_op jit(solution)/shard_map/weight_gradient/pallas_call | solution.py:722

commit v3 on v2

--- a/solution.py
+++ b/solution.py
@@ -278,17 +278,19 @@
             write(k, rows, total)
         return carry
 
-    lax.fori_loop(0, mode_block // 16, step, 0)
-
-
-def forward_planes(source, table_y, fwd_z, mid, send):
-    first_pass = dot32(table_y[...], source[...])
+    lax.fori_loop(0, mode_block // 16, step, 0, unroll=2)
+
+
+def spread_cells(first_pass, mid, first_cell):
     low = lanes_low((KY, 128))
     for pair in range(first_pass.shape[1] // 128):
         real_in = first_pass[:KY, pair * 128 : pair * 128 + 128]
         imag_in = first_pass[KY:, pair * 128 : pair * 128 + 128]
-        mid[:, 2 * pair, :] = jnp.where(low, real_in, swap(imag_in))
-        mid[:, 2 * pair + 1, :] = jnp.where(low, swap(real_in), imag_in)
+        mid[:, first_cell + 2 * pair, :] = jnp.where(low, real_in, swap(imag_in))
+        mid[:, first_cell + 2 * pair + 1, :] = jnp.where(low, swap(real_in), imag_in)
+
+
+def forward_z(fwd_z, mid, send):
     group_size, mode_block, pair_width = send.shape
     per_half = 256 // mode_block
     for half in range(2):
@@ -320,11 +322,12 @@
 
 def fused_kernel(
     cos_x, sin_x, norm_scale, group_size, sample_count, alias_count,
-    field_hbm, cot_hbm, weights_hbm, point_ref, table_y, table_y_t, fwd_z, inv_z, spread,
+    field_hbm, cot_hbm, weights_hbm, point_hbm, y_hbm, y_t_hbm, fwd_hbm, inv_hbm, spread_hbm,
     field_out, field_grad, shared_in, shared_grad,
-    field, cot, weights, folded, send, arrive, coef_in, coef_grad, mixed, mid, stacked, accum,
+    point_ref, table_y, table_y_t, fwd_z, inv_z, spread,
+    field, cot, weights, folded, send, arrive, coef_in, coef_grad, mixed, mid, mid_next, stacked, accum,
     out_block, grad_block, tail_block, point_wide, point_wide_t,
-    load_sem, weight_sem, send_sem, recv_sem, sa_send, sa_recv, own_sem,
+    load_sem, table_sem, weight_sem, send_sem, recv_sem, sa_send, sa_recv, own_sem,
 ):
     me = lax.axis_index("gx")
     mine = lax.axis_index("sa")
@@ -334,7 +337,16 @@
 
     load_field = pltpu.make_async_copy(field_hbm.at[0, 0], field, load_sem.at[0])
     load_cot = pltpu.make_async_copy(cot_hbm.at[0, 0], cot, load_sem.at[1])
+    load_tables = [
+        pltpu.make_async_copy(source, target, table_sem.at[index])
+        for index, (source, target) in enumerate((
+            (y_hbm, table_y), (fwd_hbm, fwd_z), (point_hbm, point_ref),
+            (spread_hbm, spread), (inv_hbm, inv_z), (y_t_hbm, table_y_t),
+        ))
+    ]
     load_field.start()
+    for load in load_tables:
+        load.start()
     load_cot.start()
 
     def weight_copy(kx):
@@ -374,13 +386,14 @@
         for hop in range(1, group_size):
             plane_copy(turn, hop).wait_recv()
 
-    def sample_copy(which, hop):
+    def sample_copy(which, half, hop):
         source, target = ((coef_in, shared_in), (coef_grad, shared_grad))[which]
+        span = pl.ds(half * (x_length // 2), x_length // 2)
         return pltpu.make_async_remote_copy(
-            src_ref=source,
-            dst_ref=target.at[mine],
-            send_sem=sa_send.at[which, hop],
-            recv_sem=sa_recv.at[which, hop],
+            src_ref=source.at[span],
+            dst_ref=target.at[mine, span],
+            send_sem=sa_send.at[which, half, hop],
+            recv_sem=sa_recv.at[which, half, hop],
             device_id={"sa": lax.rem(mine + hop, sample_count)},
             device_id_type=MESH,
         )
@@ -389,10 +402,11 @@
         source, target = ((coef_in, shared_in), (coef_grad, shared_grad))[which]
         return pltpu.make_async_copy(source, target.at[mine], own_sem.at[which])
 
-    def samples_start(which):
+    def samples_start(which, half):
         for hop in range(1, sample_count):
-            sample_copy(which, hop).start()
-        own_copy(which).start()
+            sample_copy(which, half, hop).start()
+        if half == 0:
+            own_copy(which).start()
 
     def forward_modes(turn, coef):
         def read(j, rows):
@@ -513,13 +527,11 @@
             columns = slice(part * 256, part * 256 + 256)
             accum[:, columns] = dot32(source[:, columns], wide[...])
 
-    def add_spectrum():
-        for part in range(accum.shape[1] // 256):
-            columns = slice(part * 256, part * 256 + 256)
-            accum[:, columns] += dot32(table_y_t[...], stacked[:, columns])
-
     load_field.wait()
-    forward_planes(field, table_y, fwd_z, mid, send.at[0])
+    load_tables[0].wait()
+    spread_cells(dot32(table_y[...], field[...]), mid, 0)
+    load_tables[1].wait()
+    forward_z(fwd_z, mid, send.at[0])
     pl.semaphore_wait(barrier, group_size + sample_count - 2)
     exchange_start(0)
 
@@ -532,6 +544,8 @@
         wide = lax.dot_general(block.astype(jnp.bfloat16), spread[...], NT, preferred_element_type=jnp.float32)
         return jnp.where(same_block, wide, 0.0).astype(jnp.bfloat16)
 
+    for load in load_tables[2:]:
+        load.wait()
     point_wide[...] = widened(dot32(spread[...], point_ref[...]))
     point_wide_t[...] = widened(
         lax.dot_general(spread[...], point_ref[...], NT, preferred_element_type=jnp.float32)
@@ -541,7 +555,7 @@
     fold_first(0)
     exchange_wait(0)
     forward_modes(0, coef_in)
-    samples_start(0)
+    samples_start(0, 0)
     lax.fori_loop(1, x_length // 2, mix_and_fold, 0)
     for group in range(groups):
         mix_in_group(x_length // 2 - 1, group)
@@ -549,38 +563,44 @@
     exchange_start(1)
     load_cot.wait()
     exchange_wait(1)
+    samples_start(0, 1)
     inverse_planes(arrive.at[1], inv_z, mid, stacked, norm_scale)
-    add_spectrum()
-
-    def activate(index, carry):
-        rows = pl.ds(pl.multiple_of(index * 16, 16), 16)
-        pre_act = accum[rows, :]
-        square = pre_act * pre_act
-        half_gate = 0.5 + 0.5 * jnp.tanh(pre_act * (ROOT_CONST + ROOT_CONST * GELU_COEF * square))
-        activated = pre_act * half_gate
-        inner_slope = 2.0 * ROOT_CONST + 6.0 * ROOT_CONST * GELU_COEF * square
-        gelu_slope = half_gate + activated * (1.0 - half_gate) * inner_slope
-        out_block[rows, :] = activated.astype(jnp.bfloat16)
-        grad_block[rows, :] = (cot[rows, :].astype(jnp.float32) * gelu_slope).astype(jnp.bfloat16)
-        return carry
-
-    lax.fori_loop(0, accum.shape[0] // 16, activate, 0)
+    for part in range(accum.shape[1] // 256):
+        columns = slice(part * 256, part * 256 + 256)
+        spectrum = dot32(table_y_t[...], stacked[:, columns])
+        for start in range(0, accum.shape[0], 32):
+            rows = slice(start, start + 32)
+            pre_act = accum[rows, columns] + spectrum[rows]
+            square = pre_act * pre_act
+            half_gate = 0.5 + 0.5 * jnp.tanh(pre_act * (ROOT_CONST + ROOT_CONST * GELU_COEF * square))
+            activated = pre_act * half_gate
+            inner_slope = 2.0 * ROOT_CONST + 6.0 * ROOT_CONST * GELU_COEF * square
+            gelu_slope = half_gate + activated * (1.0 - half_gate) * inner_slope
+            out_block[rows, columns] = activated.astype(jnp.bfloat16)
+            grad_block[rows, columns] = (cot[rows, columns].astype(jnp.float32) * gelu_slope).astype(
+                jnp.bfloat16
+            )
+        spread_cells(dot32(table_y[...], grad_block[:, columns]), mid_next, 4 * part)
+    forward_z(fwd_z, mid_next, send.at[2])
+    exchange_start(2)
     store_out = pltpu.make_async_copy(out_block, field_out.at[0, 0], load_sem.at[2])
     store_out.start()
 
-    forward_planes(grad_block, table_y, fwd_z, mid, send.at[2])
-    exchange_start(2)
     pointwise_into(grad_block, point_wide_t)
     exchange_wait(2)
     forward_modes(2, coef_grad)
-    samples_start(1)
+    samples_start(1, 0)
     lax.fori_loop(0, x_length // 2, mix_back, 0)
     inverse_modes(3)
     exchange_start(3)
+    samples_start(1, 1)
     exchange_wait(3)
     inverse_planes(arrive.at[3], inv_z, mid, stacked, norm_scale)
-    add_spectrum()
-    tail_block[...] = accum[...].astype(jnp.bfloat16)
+    for part in range(accum.shape[1] // 256):
+        columns = slice(part * 256, part * 256 + 256)
+        tail_block[:, columns] = (
+            accum[:, columns] + dot32(table_y_t[...], stacked[:, columns])
+        ).astype(jnp.bfloat16)
     store_grad = pltpu.make_async_copy(tail_block, field_grad.at[0, 0], load_sem.at[3])
     store_grad.start()
 
@@ -589,8 +609,9 @@
             plane_copy(turn, hop).wait_send()
     for which in range(2):
         own_copy(which).wait()
-        for hop in range(1, sample_count):
-            sample_copy(which, hop).wait()
+        for half in range(2):
+            for hop in range(1, sample_count):
+                sample_copy(which, half, hop).wait()
     store_out.wait()
     store_grad.wait()
 
@@ -666,11 +687,11 @@
     pair_width = 2 * channels
     norm_scale = 1.0 / math.sqrt(x_length * y_count * z_count)
     cos_x, sin_x = x_tables(kx_count, x_length)
+    tables = host_tables(y_count, z_count, channels)
     bf16, f32 = jnp.bfloat16, jnp.float32
     plane = (y_count, last_width)
     coef_shape = (x_length, mode_block, pair_width)
     anywhere = pl.BlockSpec(memory_space=pl.ANY)
-    vmem = pl.BlockSpec(memory_space=pltpu.VMEM)
     field_out, field_grad, shared_in, shared_grad = pl.pallas_call(
         functools.partial(
             fused_kernel, cos_x, sin_x, norm_scale, group_size, sample_count, kx_count // x_length
@@ -681,9 +702,11 @@
             jax.ShapeDtypeStruct((sample_count,) + coef_shape, bf16),
             jax.ShapeDtypeStruct((sample_count,) + coef_shape, bf16),
         ],
-        in_specs=[anywhere] * 3 + [vmem] * 6,
+        in_specs=[anywhere] * 9,
         out_specs=[anywhere] * 4,
         scratch_shapes=[
+            pltpu.VMEM((channels, channels), bf16),
+            *[pltpu.VMEM(table.shape, bf16) for table in tables],
             pltpu.VMEM(plane, bf16),
             pltpu.VMEM(plane, bf16),
             pltpu.VMEM((kx_count, mode_block * channels, pair_width), bf16),
@@ -694,6 +717,7 @@
             pltpu.VMEM(coef_shape, bf16),
             pltpu.VMEM(coef_shape, f32),
             pltpu.VMEM((KY, z_count, pair_width), f32),
+            pltpu.VMEM((KY, z_count, pair_width), f32),
             pltpu.VMEM((2 * KY, last_width), bf16),
             pltpu.VMEM(plane, f32),
             pltpu.VMEM(plane, bf16),
@@ -702,11 +726,12 @@
             pltpu.VMEM((256, 256), bf16),
             pltpu.VMEM((256, 256), bf16),
             pltpu.SemaphoreType.DMA((4,)),
+            pltpu.SemaphoreType.DMA((6,)),
             pltpu.SemaphoreType.DMA((kx_count,)),
             pltpu.SemaphoreType.DMA((4, group_size)),
             pltpu.SemaphoreType.DMA((4, group_size)),
-            pltpu.SemaphoreType.DMA((2, sample_count)),
-            pltpu.SemaphoreType.DMA((2, sample_count)),
+            pltpu.SemaphoreType.DMA((2, 2, sample_count)),
+            pltpu.SemaphoreType.DMA((2, 2, sample_count)),
             pltpu.SemaphoreType.DMA((2,)),
         ],
         compiler_params=pltpu.CompilerParams(
@@ -716,7 +741,7 @@
     )(
         field_in, cotangent,
         mode_weights.reshape(kx_count, mode_block * channels, pair_width),
-        point_weights, *host_tables(y_count, z_count, channels),
+        point_weights, *tables,
     )
     groups = mode_block // 16
     weight_grad, field_out, field_grad = pl.pallas_call(

time: 55.7 us -> 55.9 us (level)
  no operation moved by 1% of the time
where the time goes in v3:
time: 55.9 us; the launch traced here: 55.8 us
  Pallas kernels  55.1 us (99%)
  between operations  0.64 us (1%)
    pallas_call x1, Pallas kernels, fused_device(): pl.pallas_call(functools.partial(fused_kernel, cos_x, sin_x, norm_scale,...  47.1 us
    pallas_call x1, Pallas kernels, fused_device(): pl.pallas_call(weight_kernel, out_shape=[jax.ShapeDtypeStruct((x_length *...  8.07 us

profile of v3, /device:TPU:0, one launch (start us, length us, event | category | flops | bytes accessed | tf_op | source)
XLA Modules:
  0.0 55.8 jit_solution(13919178684028539308)
XLA Ops:
  0.6 47.1 %fourier_layer.1 = (bf16[1,1,256,1024]{3,2,1,0:T(8,128)(2,1)}, bf16[1,1,256,1024]{3,2,1,0:T(8,128)(2,1)}, bf16[4,8,64,128]{3,2,1,0:T(8,128)(2,1)}, bf16[4,8,64,128]{3,2,1,0:T(8,128)(2,1)}) custom-call(bf16[1,1,256,1024]{3,2,1,0:T(8,128)(2,1)} %field_hbm.1, bf16[1,1,256,1024]{3,2,1,0:T(8,128)(2,1)} %cot_hbm.1, bf16[32,4096,128]{2,1,0:T(8,128)(2,1)} %bitcast.2, ...), custom_call_target="tpu_custom_call" | custom-call | tf_op jit(solution)/shard_map/fourier_layer/pallas_call | solution.py:695
  47.7 8.1 %weight_gradient.1 = (f32[32,1024,128]{2,1,0:T(8,128)}, bf16[1,1,256,1024]{3,2,1,0:T(8,128)(2,1)}, bf16[1,1,256,1024]{3,2,1,0:T(8,128)(2,1)}) custom-call(bf16[4,8,64,128]{3,2,1,0:T(8,128)(2,1)} %get-tuple-element.10.left_hbm, bf16[4,8,64,128]{3,2,1,0:T(8,128)(2,1)} %get-tuple-element.11.right_hbm, bf16[1,1,256,1024]{3,2,1,0:T(8,128)(2,1)} %get-tuple-element.12.first_hbm, ...), custom_call_target="tpu_custom_call" | custom-call | tf_op jit(solution)/shard_map/weight_gradient/pallas_call | solution.py:747

commit v4 on v3

--- a/solution.py
+++ b/solution.py
@@ -435,10 +435,12 @@
             rows = pl.ds(pl.multiple_of(start + part * 128, 128), 128)
             for side in range(2):
                 residue = 2 * pair + side
-                total = weights[residue, rows, :].astype(jnp.float32)
-                for alias in range(1, alias_count):
-                    total = total + weights[residue + x_length * alias, rows, :].astype(jnp.float32)
-                folded[pair, rows, side * 128 : side * 128 + 128] = total.astype(jnp.bfloat16)
+                terms = [
+                    weights[residue + x_length * alias, rows, :] for alias in range(alias_count)
+                ]
+                while len(terms) > 1:
+                    terms = [sum(terms[k + 1 : k + 2], terms[k]) for k in range(0, len(terms), 2)]
+                folded[pair, rows, side * 128 : side * 128 + 128] = terms[0]
 
     row_index = lax.broadcasted_iota(jnp.int32, (8, 128), 0)
     low16 = lanes_low((16, 128))
@@ -644,28 +646,39 @@
     def block_copy(index):
         return pltpu.make_async_copy(blocks.at[index], weight_out.at[index], block_sem.at[index])
 
-    def step(residue, carry):
+    def operands(residue, rows):
+        left = jnp.concatenate([left_ref[s, residue, rows, :] for s in range(sample_count)], 0)
+        right = jnp.concatenate([right_ref[s, residue, rows, :] for s in range(sample_count)], 0)
+        flipped = left.astype(jnp.float32).T
+        flipped = jnp.concatenate([flipped[:64], flipped[64:]], axis=1)
+        wide = right.astype(jnp.float32)
+        stack = jnp.concatenate([wide, turned(wide)], 0).astype(jnp.bfloat16)
+        kept = jnp.concatenate(
+            [jnp.where(own_lane == mode, flipped, 0.0).astype(jnp.bfloat16) for mode in range(16)], 0
+        )
+        return kept, stack
+
+    def step(pair, carry):
         for group in range(groups):
-            index = residue * groups + group
             rows = slice(group * 16, group * 16 + 16)
-            left = jnp.concatenate([left_ref[s, residue, rows, :] for s in range(sample_count)], 0)
-            right = jnp.concatenate([right_ref[s, residue, rows, :] for s in range(sample_count)], 0)
-            flipped = left.astype(jnp.float32).T
-            flipped = jnp.concatenate([flipped[:64], flipped[64:]], axis=1)
-            wide = right.astype(jnp.float32)
-            stack = jnp.concatenate([wide, turned(wide)], 0).astype(jnp.bfloat16)
-            kept = jnp.concatenate(
-                [jnp.where(own_lane == mode, flipped, 0.0).astype(jnp.bfloat16) for mode in range(16)], 0
+            kept_a, stack_a = operands(2 * pair, rows)
+            kept_b, stack_b = operands(2 * pair + 1, rows)
+            empty = jnp.zeros_like(stack_a)
+            stack = jnp.concatenate(
+                [jnp.concatenate([stack_a, empty], 1), jnp.concatenate([empty, stack_b], 1)], 0
             )
-            blocks[index] = dot32(kept, stack)
-            block_copy(index).start()
+            product = dot32(jnp.concatenate([kept_a, kept_b], 1), stack)
+            for side in range(2):
+                index = (2 * pair + side) * groups + group
+                blocks[index] = product[:, side * 128 : side * 128 + 128]
+                block_copy(index).start()
         return carry
 
     step(0, 0)
     for fetch, copy in zip(fetches, passes):
         fetch.wait()
         copy.start()
-    lax.fori_loop(1, x_length, step, 0)
+    lax.fori_loop(1, x_length // 2, step, 0)
 
     def finish(index, carry):
         block_copy(index).wait()

time: 55.9 us -> 55.9 us (level)
  no operation moved by 1% of the time
where the time goes in v4:
time: 55.9 us; the launch traced here: 55.8 us
  Pallas kernels  55.1 us (99%)
  between operations  0.64 us (1%)
    pallas_call x1, Pallas kernels, fused_device(): pl.pallas_call(functools.partial(fused_kernel, cos_x, sin_x, norm_scale,...  46.9 us
    pallas_call x1, Pallas kernels, fused_device(): pl.pallas_call(weight_kernel, out_shape=[jax.ShapeDtypeStruct((x_length *...  8.21 us

profile of v4, /device:TPU:0, one launch (start us, length us, event | category | flops | bytes accessed | tf_op | source)
XLA Modules:
  0.0 55.8 jit_solution(1869123393106464165)
XLA Ops:
  0.6 46.9 %fourier_layer.1 = (bf16[1,1,256,1024]{3,2,1,0:T(8,128)(2,1)}, bf16[1,1,256,1024]{3,2,1,0:T(8,128)(2,1)}, bf16[4,8,64,128]{3,2,1,0:T(8,128)(2,1)}, bf16[4,8,64,128]{3,2,1,0:T(8,128)(2,1)}) custom-call(bf16[1,1,256,1024]{3,2,1,0:T(8,128)(2,1)} %field_hbm.1, bf16[1,1,256,1024]{3,2,1,0:T(8,128)(2,1)} %cot_hbm.1, bf16[32,4096,128]{2,1,0:T(8,128)(2,1)} %bitcast.2, ...), custom_call_target="tpu_custom_call" | custom-call | tf_op jit(solution)/shard_map/fourier_layer/pallas_call | solution.py:708
  47.5 8.2 %weight_gradient.1 = (f32[32,1024,128]{2,1,0:T(8,128)}, bf16[1,1,256,1024]{3,2,1,0:T(8,128)(2,1)}, bf16[1,1,256,1024]{3,2,1,0:T(8,128)(2,1)}) custom-call(bf16[4,8,64,128]{3,2,1,0:T(8,128)(2,1)} %get-tuple-element.10.left_hbm, bf16[4,8,64,128]{3,2,1,0:T(8,128)(2,1)} %get-tuple-element.11.right_hbm, bf16[1,1,256,1024]{3,2,1,0:T(8,128)(2,1)} %get-tuple-element.12.first_hbm, ...), custom_call_target="tpu_custom_call" | custom-call | tf_op jit(solution)/shard_map/weight_gradient/pallas_call | solution.py:760

commit v5 on v4

--- a/solution.py
+++ b/solution.py
@@ -325,7 +325,7 @@
     field_hbm, cot_hbm, weights_hbm, point_hbm, y_hbm, y_t_hbm, fwd_hbm, inv_hbm, spread_hbm,
     field_out, field_grad, shared_in, shared_grad,
     point_ref, table_y, table_y_t, fwd_z, inv_z, spread,
-    field, cot, weights, folded, send, arrive, coef_in, coef_grad, mixed, mid, mid_next, stacked, accum,
+    field, cot, weights, folded, send, arrive, gathered_coefs, mixed, mid, mid_next, stacked, accum,
     out_block, grad_block, tail_block, point_wide, point_wide_t,
     load_sem, table_sem, weight_sem, send_sem, recv_sem, sa_send, sa_recv, own_sem,
 ):
@@ -386,27 +386,56 @@
         for hop in range(1, group_size):
             plane_copy(turn, hop).wait_recv()
 
-    def sample_copy(which, half, hop):
-        source, target = ((coef_in, shared_in), (coef_grad, shared_grad))[which]
-        span = pl.ds(half * (x_length // 2), x_length // 2)
+    coef_in = gathered_coefs.at[0, mine]
+    coef_grad = gathered_coefs.at[1, mine]
+    last = sample_count - 1
+
+    def line_copy(which, way, step, slot):
+        target = lax.rem(mine + (1, last)[way], sample_count)
         return pltpu.make_async_remote_copy(
-            src_ref=source.at[span],
-            dst_ref=target.at[mine, span],
-            send_sem=sa_send.at[which, half, hop],
-            recv_sem=sa_recv.at[which, half, hop],
-            device_id={"sa": lax.rem(mine + hop, sample_count)},
+            src_ref=gathered_coefs.at[which, slot],
+            dst_ref=gathered_coefs.at[which, slot],
+            send_sem=sa_send.at[which, way, step],
+            recv_sem=sa_recv.at[which, way, step],
+            device_id={"sa": target},
             device_id_type=MESH,
         )
 
-    def own_copy(which):
-        source, target = ((coef_in, shared_in), (coef_grad, shared_grad))[which]
-        return pltpu.make_async_copy(source, target.at[mine], own_sem.at[which])
-
-    def samples_start(which, half):
-        for hop in range(1, sample_count):
-            sample_copy(which, half, hop).start()
-        if half == 0:
-            own_copy(which).start()
+    def line_step(which, step):
+        @pl.when(mine >= step)
+        def from_below():
+            slot = lax.rem(mine + sample_count - step, sample_count)
+            if step > 0:
+                line_copy(which, 0, step - 1, slot).wait_recv()
+            if step < last:
+                @pl.when(mine < last)
+                def onward():
+                    line_copy(which, 0, step, slot).start()
+
+        @pl.when(mine + step <= last)
+        def from_above():
+            slot = lax.rem(mine + step, sample_count)
+            if step > 0:
+                line_copy(which, 1, step - 1, slot).wait_recv()
+            if step < last:
+                @pl.when(mine > 0)
+                def onward():
+                    line_copy(which, 1, step, slot).start()
+
+    def line_finish(which):
+        for step in range(last):
+            @pl.when((mine >= step) & (mine < last))
+            def sent_up():
+                line_copy(which, 0, step, lax.rem(mine + sample_count - step, sample_count)).wait_send()
+
+            @pl.when((mine + step <= last) & (mine > 0))
+            def sent_down():
+                line_copy(which, 1, step, lax.rem(mine + step, sample_count)).wait_send()
+
+    def share(which):
+        return pltpu.make_async_copy(
+            gathered_coefs.at[which], (shared_in, shared_grad)[which], own_sem.at[which]
+        )
 
     def forward_modes(turn, coef):
         def read(j, rows):
@@ -557,15 +586,15 @@
     fold_first(0)
     exchange_wait(0)
     forward_modes(0, coef_in)
-    samples_start(0, 0)
+    line_step(0, 0)
     lax.fori_loop(1, x_length // 2, mix_and_fold, 0)
     for group in range(groups):
         mix_in_group(x_length // 2 - 1, group)
+    line_step(0, 1)
     inverse_modes(1)
     exchange_start(1)
     load_cot.wait()
     exchange_wait(1)
-    samples_start(0, 1)
     inverse_planes(arrive.at[1], inv_z, mid, stacked, norm_scale)
     for part in range(accum.shape[1] // 256):
         columns = slice(part * 256, part * 256 + 256)
@@ -585,18 +614,23 @@
         spread_cells(dot32(table_y[...], grad_block[:, columns]), mid_next, 4 * part)
     forward_z(fwd_z, mid_next, send.at[2])
     exchange_start(2)
+    line_step(0, 2)
     store_out = pltpu.make_async_copy(out_block, field_out.at[0, 0], load_sem.at[2])
     store_out.start()
 
     pointwise_into(grad_block, point_wide_t)
     exchange_wait(2)
     forward_modes(2, coef_grad)
-    samples_start(1, 0)
+    line_step(1, 0)
     lax.fori_loop(0, x_length // 2, mix_back, 0)
     inverse_modes(3)
     exchange_start(3)
-    samples_start(1, 1)
+    line_step(1, 1)
     exchange_wait(3)
+    line_step(1, 2)
+    for step in range(3, sample_count):
+        line_step(0, step)
+    share(0).start()
     inverse_planes(arrive.at[3], inv_z, mid, stacked, norm_scale)
     for part in range(accum.shape[1] // 256):
         columns = slice(part * 256, part * 256 + 256)
@@ -609,11 +643,12 @@
     for turn in range(4):
         for hop in range(1, group_size):
             plane_copy(turn, hop).wait_send()
+    for step in range(3, sample_count):
+        line_step(1, step)
+    share(1).start()
     for which in range(2):
-        own_copy(which).wait()
-        for half in range(2):
-            for hop in range(1, sample_count):
-                sample_copy(which, half, hop).wait()
+        line_finish(which)
+        share(which).wait()
     store_out.wait()
     store_grad.wait()
 
@@ -726,8 +761,7 @@
             pltpu.VMEM((x_length // 2, mode_block * channels, 2 * pair_width), bf16),
             pltpu.VMEM((4,) + coef_shape, bf16),
             pltpu.VMEM((4,) + coef_shape, bf16),
-            pltpu.VMEM(coef_shape, bf16),
-            pltpu.VMEM(coef_shape, bf16),
+            pltpu.VMEM((2, sample_count) + coef_shape, bf16),
             pltpu.VMEM(coef_shape, f32),
             pltpu.VMEM((KY, z_count, pair_width), f32),
             pltpu.VMEM((KY, z_count, pair_width), f32),

time: 55.9 us -> 57.4 us (1.027)
  Pallas kernels: 55.1 us -> 56.6 us
    pallas_call x1, Pallas kernels: 46.9 us -> 48.4 us  [fused_device(): pl.pallas_call(functools.partial(fused_kernel, cos_x, sin_x, norm_scale,...]
where the time goes in v5:
time: 57.4 us; the launch traced here: 57.3 us
  Pallas kernels  56.6 us (99%)
  between operations  0.64 us (1%)
    pallas_call x1, Pallas kernels, fused_device(): pl.pallas_call(functools.partial(fused_kernel, cos_x, sin_x, norm_scale,...  48.4 us
    pallas_call x1, Pallas kernels, fused_device(): pl.pallas_call(weight_kernel, out_shape=[jax.ShapeDtypeStruct((x_length *...  8.21 us

profile of v5, /device:TPU:0, one launch (start us, length us, event | category | flops | bytes accessed | tf_op | source)
XLA Modules:
  0.0 57.3 jit_solution(387196659973208425)
XLA Ops:
  0.6 48.4 %fourier_layer.1 = (bf16[1,1,256,1024]{3,2,1,0:T(8,128)(2,1)}, bf16[1,1,256,1024]{3,2,1,0:T(8,128)(2,1)}, bf16[4,8,64,128]{3,2,1,0:T(8,128)(2,1)}, bf16[4,8,64,128]{3,2,1,0:T(8,128)(2,1)}) custom-call(bf16[1,1,256,1024]{3,2,1,0:T(8,128)(2,1)} %field_hbm.1, bf16[1,1,256,1024]{3,2,1,0:T(8,128)(2,1)} %cot_hbm.1, bf16[32,4096,128]{2,1,0:T(8,128)(2,1)} %bitcast.2, ...), custom_call_target="tpu_custom_call" | custom-call | tf_op jit(solution)/shard_map/fourier_layer/pallas_call | solution.py:743
  49.0 8.2 %weight_gradient.1 = (f32[32,1024,128]{2,1,0:T(8,128)}, bf16[1,1,256,1024]{3,2,1,0:T(8,128)(2,1)}, bf16[1,1,256,1024]{3,2,1,0:T(8,128)(2,1)}) custom-call(bf16[4,8,64,128]{3,2,1,0:T(8,128)(2,1)} %get-tuple-element.10.left_hbm, bf16[4,8,64,128]{3,2,1,0:T(8,128)(2,1)} %get-tuple-element.11.right_hbm, bf16[1,1,256,1024]{3,2,1,0:T(8,128)(2,1)} %get-tuple-element.12.first_hbm, ...), custom_call_target="tpu_custom_call" | custom-call | tf_op jit(solution)/shard_map/weight_gradient/pallas_call | solution.py:794

commit v6 on v4

--- a/solution.py
+++ b/solution.py
@@ -325,7 +325,7 @@
     field_hbm, cot_hbm, weights_hbm, point_hbm, y_hbm, y_t_hbm, fwd_hbm, inv_hbm, spread_hbm,
     field_out, field_grad, shared_in, shared_grad,
     point_ref, table_y, table_y_t, fwd_z, inv_z, spread,
-    field, cot, weights, folded, send, arrive, coef_in, coef_grad, mixed, mid, mid_next, stacked, accum,
+    field, cot, weights, folded, folded_t, send, arrive, coef_in, coef_grad, mixed, mid, mid_next, stacked, accum,
     out_block, grad_block, tail_block, point_wide, point_wide_t,
     load_sem, table_sem, weight_sem, send_sem, recv_sem, sa_send, sa_recv, own_sem,
 ):
@@ -432,7 +432,7 @@
 
     def fold_rows(pair, start):
         for part in range(1024 // 128):
-            rows = pl.ds(pl.multiple_of(start + part * 128, 128), 128)
+            rows = slice(start + part * 128, start + part * 128 + 128)
             for side in range(2):
                 residue = 2 * pair + side
                 terms = [
@@ -440,7 +440,9 @@
                 ]
                 while len(terms) > 1:
                     terms = [sum(terms[k + 1 : k + 2], terms[k]) for k in range(0, len(terms), 2)]
-                folded[pair, rows, side * 128 : side * 128 + 128] = terms[0]
+                columns = slice(side * 128, side * 128 + 128)
+                folded[pair, rows, columns] = terms[0]
+                folded_t[pair, columns, rows] = terms[0].T
 
     row_index = lax.broadcasted_iota(jnp.int32, (8, 128), 0)
     low16 = lanes_low((16, 128))
@@ -490,11 +492,8 @@
     def fold_first(pair):
         wait_pair(pair)
 
-        def step(index, inner):
-            fold_rows(pair, index * 1024)
-            return inner
-
-        lax.fori_loop(0, groups, step, 0)
+        for group in range(groups):
+            fold_rows(pair, group * 1024)
 
     def mix_and_fold(pair, carry):
         wait_pair(pair)
@@ -512,9 +511,8 @@
                 coef = coef_grad[2 * pair + side, rows, :].astype(jnp.float32)
                 both = jnp.concatenate([coef, turned(coef)], 0).astype(jnp.bfloat16)
                 parts.append(jnp.concatenate([both, empty] if side == 0 else [empty, both], 1))
-            product = lax.dot_general(
-                jnp.concatenate(parts, 0), folded[pair, group * 1024 : group * 1024 + 1024, :],
-                NT, preferred_element_type=jnp.float32,
+            product = dot32(
+                jnp.concatenate(parts, 0), folded_t[pair, :, group * 1024 : group * 1024 + 1024]
             )
             for side in range(2):
                 start = side * 32
@@ -620,7 +618,7 @@
 
 def weight_kernel(
     left_hbm, right_hbm, first_hbm, second_hbm, weight_out, first_out, second_out,
-    left_ref, right_ref, first_ref, second_ref, blocks, load_sem, pass_sem, block_sem,
+    left_ref, right_ref, first_ref, second_ref, masks, blocks, load_sem, pass_sem, block_sem,
 ):
     loads = [
         pltpu.make_async_copy(left_hbm, left_ref, load_sem.at[0]),
@@ -642,6 +640,8 @@
     depth = 2 * sample_count * 16
     groups = mode_block // 16
     own_lane = lax.broadcasted_iota(jnp.int32, (64, depth), 1) % 16
+    for mode in range(16):
+        masks[mode] = jnp.where(own_lane == mode, 1.0, 0.0).astype(jnp.bfloat16)
 
     def block_copy(index):
         return pltpu.make_async_copy(blocks.at[index], weight_out.at[index], block_sem.at[index])
@@ -650,11 +650,11 @@
         left = jnp.concatenate([left_ref[s, residue, rows, :] for s in range(sample_count)], 0)
         right = jnp.concatenate([right_ref[s, residue, rows, :] for s in range(sample_count)], 0)
         flipped = left.astype(jnp.float32).T
-        flipped = jnp.concatenate([flipped[:64], flipped[64:]], axis=1)
+        flipped = jnp.concatenate([flipped[:64], flipped[64:]], axis=1).astype(jnp.bfloat16)
         wide = right.astype(jnp.float32)
         stack = jnp.concatenate([wide, turned(wide)], 0).astype(jnp.bfloat16)
         kept = jnp.concatenate(
-            [jnp.where(own_lane == mode, flipped, 0.0).astype(jnp.bfloat16) for mode in range(16)], 0
+            [flipped * masks[mode] for mode in range(16)], 0
         )
         return kept, stack
 
@@ -724,6 +724,7 @@
             pltpu.VMEM(plane, bf16),
             pltpu.VMEM((kx_count, mode_block * channels, pair_width), bf16),
             pltpu.VMEM((x_length // 2, mode_block * channels, 2 * pair_width), bf16),
+            pltpu.VMEM((x_length // 2, 2 * pair_width, mode_block * channels), bf16),
             pltpu.VMEM((4,) + coef_shape, bf16),
             pltpu.VMEM((4,) + coef_shape, bf16),
             pltpu.VMEM(coef_shape, bf16),
@@ -748,7 +749,7 @@
             pltpu.SemaphoreType.DMA((2,)),
         ],
         compiler_params=pltpu.CompilerParams(
-            collective_id=0, has_side_effects=True, vmem_limit_bytes=56 * 1024 * 1024
+            collective_id=0, has_side_effects=True, vmem_limit_bytes=60 * 1024 * 1024
         ),
         name="fourier_layer",
     )(
@@ -771,6 +772,7 @@
             pltpu.VMEM((sample_count,) + coef_shape, bf16),
             pltpu.VMEM((1, 1) + plane, bf16),
             pltpu.VMEM((1, 1) + plane, bf16),
+            pltpu.VMEM((16, channels, 2 * sample_count * 16), bf16),
             pltpu.VMEM((x_length * groups, 16 * channels, pair_width), f32),
             pltpu.SemaphoreType.DMA((4,)),
             pltpu.SemaphoreType.DMA((2,)),

time: 55.9 us -> 57.2 us (1.023)
  Pallas kernels: 55.1 us -> 56.4 us
    pallas_call x1, Pallas kernels: 46.9 us -> 48.2 us  [fused_device(): pl.pallas_call(functools.partial(fused_kernel, cos_x, sin_x, norm_scale,...]
where the time goes in v6:
time: 57.2 us; the launch traced here: 57.1 us
  Pallas kernels  56.4 us (99%)
  between operations  0.64 us (1%)
    pallas_call x1, Pallas kernels, fused_device(): pl.pallas_call(functools.partial(fused_kernel, cos_x, sin_x, norm_scale,...  48.2 us
    pallas_call x1, Pallas kernels, fused_device(): pl.pallas_call(weight_kernel, out_shape=[jax.ShapeDtypeStruct((x_length *...  8.22 us

profile of v6, /device:TPU:0, one launch (start us, length us, event | category | flops | bytes accessed | tf_op | source)
XLA Modules:
  0.0 57.1 jit_solution(11218319988039409322)
XLA Ops:
  0.6 48.2 %fourier_layer.1 = (bf16[1,1,256,1024]{3,2,1,0:T(8,128)(2,1)}, bf16[1,1,256,1024]{3,2,1,0:T(8,128)(2,1)}, bf16[4,8,64,128]{3,2,1,0:T(8,128)(2,1)}, bf16[4,8,64,128]{3,2,1,0:T(8,128)(2,1)}) custom-call(bf16[1,1,256,1024]{3,2,1,0:T(8,128)(2,1)} %field_hbm.1, bf16[1,1,256,1024]{3,2,1,0:T(8,128)(2,1)} %cot_hbm.1, bf16[32,4096,128]{2,1,0:T(8,128)(2,1)} %bitcast.2, ...), custom_call_target="tpu_custom_call" | custom-call | tf_op jit(solution)/shard_map/fourier_layer/pallas_call | solution.py:708
  48.9 8.2 %weight_gradient.1 = (f32[32,1024,128]{2,1,0:T(8,128)}, bf16[1,1,256,1024]{3,2,1,0:T(8,128)(2,1)}, bf16[1,1,256,1024]{3,2,1,0:T(8,128)(2,1)}) custom-call(bf16[4,8,64,128]{3,2,1,0:T(8,128)(2,1)} %get-tuple-element.10.left_hbm, bf16[4,8,64,128]{3,2,1,0:T(8,128)(2,1)} %get-tuple-element.11.right_hbm, bf16[1,1,256,1024]{3,2,1,0:T(8,128)(2,1)} %get-tuple-element.12.first_hbm, ...), custom_call_target="tpu_custom_call" | custom-call | tf_op jit(solution)/shard_map/weight_gradient/pallas_call | solution.py:761
